TPU v7x, 32 devices: a whole 2x2x4 slice. The times are simulated.
32 devices in a mesh: wide: 16 (over z, y, x), narrow: 2 (over core).
Axes of the slice: x: 2, y: 2, z: 4, core: 2. Of those that a mesh axis runs over, the one named last changes fastest.
Arguments:
- inputs: bfloat16 [32768, 768], P('wide'), may hold values from -6 to 6
- segments: int32 [32768], P('wide'), may hold values from 0 to 3, as said below
- valid: int32 [32768], P('wide'), may hold values from 0 to 1, as said below
- w_query: bfloat16 [768, 768], P(None, 'narrow'), may hold values from -0.21875 to 0.21875
- w_key: bfloat16 [768, 768], P(None, 'narrow'), may hold values from -0.21875 to 0.21875
- w_value: bfloat16 [768, 768], P(None, 'narrow'), may hold values from -0.21875 to 0.21875
- b_query: bfloat16 [768], P('narrow'), may hold values from -3 to 3
- b_value: bfloat16 [768], P('narrow'), may hold values from -3 to 3
- w_attn_out: bfloat16 [768, 768], P('narrow'), may hold values from -1.75 to 1.75
- b_attn_out: bfloat16 [768], replicated, may hold values from -3 to 3
- gain_one: bfloat16 [768], replicated, may hold values from 0.099609375 to 1.8984375
- shift_one: bfloat16 [768], replicated, may hold values from -3 to 3
- w_ffn_in: bfloat16 [768, 3072], P(None, 'narrow'), may hold values from -0.21875 to 0.21875
- b_ffn_in: bfloat16 [3072], P('narrow'), may hold values from -3 to 3
- w_ffn_out: bfloat16 [3072, 768], P('narrow'), may hold values from -0.109375 to 0.109375
- b_ffn_out: bfloat16 [768], replicated, may hold values from -3 to 3
- gain_two: bfloat16 [768], replicated, may hold values from 0.099609375 to 1.8984375
- shift_two: bfloat16 [768], replicated, may hold values from -3 to 3
- out_grad: bfloat16 [32768, 768], P('wide'), may hold values from -18 to 18
Outputs:
- output: bfloat16 [32768, 768], P('wide')
- input_grad: bfloat16 [32768, 768], P('wide')
- grad_w_query: float32 [768, 768], P(None, 'narrow')
- grad_w_key: float32 [768, 768], P(None, 'narrow')
- grad_w_value: float32 [768, 768], P(None, 'narrow')
- grad_b_query: float32 [768], P('narrow')
- grad_b_value: float32 [768], P('narrow')
- grad_w_attn_out: float32 [768, 768], P('narrow')
- grad_b_attn_out: float32 [768], replicated
- grad_gain_one: float32 [768], replicated
- grad_shift_one: float32 [768], replicated
- grad_w_ffn_in: float32 [768, 3072], P(None, 'narrow')
- grad_b_ffn_in: float32 [3072], P('narrow')
- grad_w_ffn_out: float32 [3072, 768], P('narrow')
- grad_b_ffn_out: float32 [768], replicated
- grad_gain_two: float32 [768], replicated
- grad_shift_two: float32 [768], replicated
- rms: float32 [4], replicated
Inputs may be any that keep to these rules, and one draw needn't show every extreme that they name: `segments`: each packed row of 512 tokens holds exactly four documents: the segment numbers start at 0 and rise by one at each new document; no document starts in the last quarter of a row. In each packed row the valid tokens are a prefix; fewer than 64 slots at the end of a row are padding.
All inputs are finite; a program needn't handle non-finite values.
Results may differ from a plain program's by a relative error of at most 0.015.
Values may be sent and summed in bfloat16 or wider, within the bound.
No kernel may reach another device: no remote copies, remote signals or barrier semaphores. Data moves between devices by JAX's collectives and lax.ppermute only.
A program may use at most 192 MiB of HBM per device.

v0:
```python
from functools import partial

import jax
import jax.numpy as jnp
from jax import lax
from jax.sharding import PartitionSpec as P

D = 768
HEAD_DIM = 64
SEQ_LEN = 512


norm_eps = 1e-06


def left_contract(left, right):
    return lax.dot_general(
        left, right, (((0,), (0,)), ((), ())), preferred_element_type=jnp.float32
    )


def right_contract(left, right):
    return lax.dot_general(
        left, right, (((1,), (1,)), ((), ())), preferred_element_type=jnp.float32
    )


def keep_same(values):
    return values


def layer_norm(values, gain, shift):
    centred = values - jnp.mean(values, axis=-1, keepdims=True)
    inverse = lax.rsqrt(jnp.mean(centred * centred, axis=-1, keepdims=True) + norm_eps)
    normed = centred * inverse
    return (normed * gain + shift, normed, inverse)


def norm_back(grad_rows, normed, inverse, gain):
    inner = grad_rows * gain
    centre_part = jnp.mean(inner, axis=-1, keepdims=True)
    slope_part = jnp.mean(inner * normed, axis=-1, keepdims=True)
    return inverse * (inner - centre_part - normed * slope_part)


def masked_scores(queries, key_rows, seg_row, valid_row, scale):
    scores = (
        jnp.einsum("qhd,khd->hqk", queries, key_rows, preferred_element_type=jnp.float32) * scale
    )
    allowed = (seg_row[:, None] == seg_row[None, :]) & (valid_row[None, :] == 1)
    return jnp.where(allowed[None], scores, -1e30)


def attend_forward(packed, scale):
    queries, key_rows, value_rows, seg_row, valid_row = packed
    scores = masked_scores(queries, key_rows, seg_row, valid_row, scale)
    peak = jnp.max(scores, axis=-1, keepdims=True)
    shifted = jnp.exp(scores - peak)
    totals = jnp.sum(shifted, axis=-1, keepdims=True)
    weights = (shifted / totals).astype(jnp.bfloat16)
    context = jnp.einsum("hqk,khd->qhd", weights, value_rows, preferred_element_type=jnp.float32)
    return (context.astype(jnp.bfloat16), peak + jnp.log(totals))


def attend_backward(packed, scale):
    queries, key_rows, value_rows, seg_row, valid_row, log_totals, grad_context = packed
    probs = jnp.exp(masked_scores(queries, key_rows, seg_row, valid_row, scale) - log_totals)
    grad_probs = jnp.einsum(
        "qhd,khd->hqk", grad_context, value_rows, preferred_element_type=jnp.float32
    )
    centred = grad_probs - jnp.sum(grad_probs * probs, axis=-1, keepdims=True)
    grad_scores = (probs * centred).astype(jnp.bfloat16)
    grad_queries = (
        jnp.einsum("hqk,khd->qhd", grad_scores, key_rows, preferred_element_type=jnp.float32)
        * scale
    )
    grad_keys = (
        jnp.einsum("hqk,qhd->khd", grad_scores, queries, preferred_element_type=jnp.float32) * scale
    )
    grad_values = jnp.einsum(
        "hqk,qhd->khd", probs.astype(jnp.bfloat16), grad_context, preferred_element_type=jnp.float32
    )
    return (
        grad_queries.astype(jnp.bfloat16),
        grad_keys.astype(jnp.bfloat16),
        grad_values.astype(jnp.bfloat16),
    )


def run_layer(
    hidden_in, seg_rows, valid_rows, cotangent, weights, reducers, widen_rows, share_rows
):
    (
        w_query,
        w_key,
        w_value,
        b_query,
        b_value,
        w_attn_out,
        b_attn_out,
        gain_one,
        shift_one,
        w_ffn_in,
        b_ffn_in,
        w_ffn_out,
        b_ffn_out,
        gain_two,
        shift_two,
    ) = weights
    sum_attn, sum_ffn, sum_hidden, sum_input = reducers
    f32 = jnp.float32
    row_count = hidden_in.shape[0]
    head_width = w_query.shape[1]
    heads_here = head_width // HEAD_DIM
    seq_count = row_count // SEQ_LEN
    scale = HEAD_DIM ** (-0.5)

    def split_heads(array):
        return array.reshape(seq_count, SEQ_LEN, heads_here, HEAD_DIM)

    queries = (
        jnp.dot(hidden_in, w_query, preferred_element_type=f32) + b_query.astype(f32)
    ).astype(jnp.bfloat16)
    key_rows = jnp.dot(hidden_in, w_key, preferred_element_type=f32).astype(jnp.bfloat16)
    value_rows = (
        jnp.dot(hidden_in, w_value, preferred_element_type=f32) + b_value.astype(f32)
    ).astype(jnp.bfloat16)
    seg_block = seg_rows.reshape(seq_count, SEQ_LEN)
    valid_block = valid_rows.reshape(seq_count, SEQ_LEN)
    head_inputs = (
        split_heads(queries),
        split_heads(key_rows),
        split_heads(value_rows),
        seg_block,
        valid_block,
    )
    context, log_totals = lax.map(partial(attend_forward, scale=scale), head_inputs)
    context = context.reshape(row_count, head_width)
    attn = sum_attn(jnp.dot(context, w_attn_out, preferred_element_type=f32)) + b_attn_out.astype(
        f32
    )
    mixed = share_rows(hidden_in).astype(f32) + attn
    first, normed_one, inverse_one = layer_norm(mixed, gain_one.astype(f32), shift_one.astype(f32))
    first_low = widen_rows(first.astype(jnp.bfloat16))
    pre_act = jnp.dot(first_low, w_ffn_in, preferred_element_type=f32) + b_ffn_in.astype(f32)
    activated = jax.nn.gelu(pre_act, approximate=False).astype(jnp.bfloat16)
    ffn_out = sum_ffn(jnp.dot(activated, w_ffn_out, preferred_element_type=f32)) + b_ffn_out.astype(
        f32
    )
    second = first + ffn_out
    final, normed_two, inverse_two = layer_norm(second, gain_two.astype(f32), shift_two.astype(f32))
    valid_float = share_rows(valid_rows).astype(f32)
    grad_out = share_rows(cotangent).astype(f32) * valid_float[:, None]
    d_gain_two = jnp.sum(grad_out * normed_two, axis=0)
    d_shift_two = jnp.sum(grad_out, axis=0)
    grad_second = norm_back(grad_out, normed_two, inverse_two, gain_two.astype(f32))
    d_b_ffn_out = jnp.sum(grad_second, axis=0)
    low_second = widen_rows(grad_second.astype(jnp.bfloat16))
    d_w_ffn_out = left_contract(activated, low_second)
    grad_act = right_contract(low_second, w_ffn_out)
    unused_value, gelu_back = jax.vjp(partial(jax.nn.gelu, approximate=False), pre_act)
    grad_pre = gelu_back(grad_act)[0].astype(jnp.bfloat16)
    d_b_ffn_in = jnp.sum(grad_pre.astype(f32), axis=0)
    d_w_ffn_in = left_contract(first_low, grad_pre)
    grad_first = grad_second + sum_hidden(right_contract(grad_pre, w_ffn_in))
    d_gain_one = jnp.sum(grad_first * normed_one, axis=0)
    d_shift_one = jnp.sum(grad_first, axis=0)
    grad_mixed = norm_back(grad_first, normed_one, inverse_one, gain_one.astype(f32))
    d_b_attn_out = jnp.sum(grad_mixed, axis=0)
    low_mixed = widen_rows(grad_mixed.astype(jnp.bfloat16))
    d_w_attn_out = left_contract(context, low_mixed)
    grad_context = right_contract(low_mixed, w_attn_out).astype(jnp.bfloat16)
    back_inputs = head_inputs + (log_totals, split_heads(grad_context))
    grad_queries, grad_keys, grad_values = lax.map(
        partial(attend_backward, scale=scale), back_inputs
    )
    grad_queries = grad_queries.reshape(row_count, head_width)
    grad_keys = grad_keys.reshape(row_count, head_width)
    grad_values = grad_values.reshape(row_count, head_width)
    d_b_query = jnp.sum(grad_queries.astype(f32), axis=0)
    d_b_value = jnp.sum(grad_values.astype(f32), axis=0)
    d_w_query = left_contract(hidden_in, grad_queries)
    d_w_key = left_contract(hidden_in, grad_keys)
    d_w_value = left_contract(hidden_in, grad_values)
    partial_in = (
        right_contract(grad_queries, w_query)
        + right_contract(grad_keys, w_key)
        + right_contract(grad_values, w_value)
    )
    grad_in = grad_mixed + sum_input(partial_in)
    stats = jnp.stack(
        [
            jnp.sum(valid_float * jnp.sum(g * g, axis=-1))
            for g in (grad_in, grad_second, grad_first, grad_mixed)
        ]
        + [jnp.sum(valid_float)]
    )
    sharded = (
        d_w_query,
        d_w_key,
        d_w_value,
        d_w_ffn_in,
        d_b_query,
        d_b_value,
        d_b_ffn_in,
        d_w_attn_out,
        d_w_ffn_out,
    )
    replicated = (d_b_attn_out, d_gain_one, d_shift_one, d_b_ffn_out, d_gain_two, d_shift_two)
    return (final.astype(jnp.bfloat16), grad_in.astype(jnp.bfloat16), sharded, replicated, stats)


def body(
    inputs,
    segments,
    valid,
    w_query,
    w_key,
    w_value,
    b_query,
    b_value,
    w_attn_out,
    b_attn_out,
    gain_one,
    shift_one,
    w_ffn_in,
    b_ffn_in,
    w_ffn_out,
    b_ffn_out,
    gain_two,
    shift_two,
    out_grad,
):
    weights = (
        w_query,
        w_key,
        w_value,
        b_query,
        b_value,
        w_attn_out,
        b_attn_out,
        gain_one,
        shift_one,
        w_ffn_in,
        b_ffn_in,
        w_ffn_out,
        b_ffn_out,
        gain_two,
        shift_two,
    )

    def sum_attn(values):
        return lax.psum(values, "narrow")

    def sum_ffn(values):
        return lax.psum(values, "narrow")

    def sum_hidden(values):
        return lax.psum(values, "narrow")

    def sum_input(values):
        return lax.psum(values.astype(jnp.bfloat16), "narrow").astype(jnp.float32)

    output, input_grad, sharded, replicated, stats = run_layer(
        inputs,
        segments,
        valid,
        out_grad,
        weights,
        (sum_attn, sum_ffn, sum_hidden, sum_input),
        keep_same,
        keep_same,
    )
    extra_members = ()
    summed = lax.psum(sharded + replicated + extra_members, "wide")
    stat_total = lax.psum(stats, "wide")
    rms = jnp.sqrt(stat_total[:4] / (stat_total[4] * D))
    return (
        output,
        input_grad,
        summed[0],
        summed[1],
        summed[2],
        summed[4],
        summed[5],
        summed[7],
        summed[9],
        summed[10],
        summed[11],
        summed[3],
        summed[6],
        summed[8],
        summed[12],
        summed[13],
        summed[14],
        rms,
    )


def solution(mesh):
    in_specs = (
        P("wide", None),
        P("wide"),
        P("wide"),
        P(None, "narrow"),
        P(None, "narrow"),
        P(None, "narrow"),
        P("narrow"),
        P("narrow"),
        P("narrow", None),
        P(),
        P(),
        P(),
        P(None, "narrow"),
        P("narrow"),
        P("narrow", None),
        P(),
        P(),
        P(),
        P("wide", None),
    )
    out_specs = (
        P("wide", None),
        P("wide", None),
        P(None, "narrow"),
        P(None, "narrow"),
        P(None, "narrow"),
        P("narrow"),
        P("narrow"),
        P("narrow", None),
        P(),
        P(),
        P(),
        P(None, "narrow"),
        P("narrow"),
        P("narrow", None),
        P(),
        P(),
        P(),
        P(),
    )
    return jax.shard_map(body, mesh=mesh, in_specs=in_specs, out_specs=out_specs, check_vma=False)
```

profile of v0, /device:TPU:0, one launch (start us, length us, event | category | flops | bytes accessed | tf_op | source)
XLA Modules:
  0.0 881.6 jit_solution(1204482865008185454)
XLA Ops:
  8.1 5.0 add_convert_fusion.4
  22.4 4.8 add_convert_fusion.3
  36.7 4.8 convolution_convert_fusion.1
  52.2 33.1 %while.26 = (s32[]{:T(128)}, bf16[4,512,6,64]{1,3,2,0:T(8,128)(2,1)}, f32[4,6,512,1]{2,1,3,0:T(8,128)}, bf16[4,512,6,64]{1,3,2,0:T(8,128)(2,1)}, s32[4,512]{1,0:...) while((s32[]{:T(128)}, ...), condition=%wide.region_3.4_spmd, body=%wide.region_0.3_spmd.sunk | while | flops 422245888 | bytes 21610084 | solution.py:137
  94.4 34.7 %all-reduce.8.cloned.1.call-done = f32[2048,768]{1,0:T(8,128)} async-done(((f32[2048,768]{1,0:T(8,128)}), f32[2048,768]{1,0:T(8,128)}) %all-reduce.8.cloned.1.call-update) | async-done | bytes 6291472 | tf_op jit(solution)/shard_map/psum | solution.py:253
  134.6 34.1 %multiply_convert_fusion.1 = (bf16[2048,1536]{1,0:T(8,128)(2,1)S(1)}, f32[2048,1536]{1,0:T(8,128)}, f32[2048,1536]{1,0:T(8,128)}) fusion(f32[1536]{0:T(1024)S(1)} %convert_element_type.131, bf16[768,1536]{1,0:T(8,128)(2,1)S(1)} %copy-done, f32[2048,768]{1,0:T(8,128)S(1)} %get-tuple-element.282, f32[768]{0:T(1024)S(1)} %convert_element_type.129, ...), kind=kOutput, calls=%fused_computation.73 | convolution fusion | flops 5047320576 | bytes 40136704 | tf_op jit(solution)/shard_map/dot_general | solution.py:145
  171.4 6.8 fusion.84
  178.9 32.6 %all-reduce.10.cloned.1.call-done = f32[2048,768]{1,0:T(8,128)} async-done(((f32[2048,768]{1,0:T(8,128)}), f32[2048,768]{1,0:T(8,128)}) %all-reduce.10.cloned.1.call-update) | async-done | bytes 6291472 | tf_op jit(solution)/shard_map/psum | solution.py:256
  211.6 6.1 fusion.80
  223.8 6.4 multiply_reduce_fusion.3
  230.2 20.4 %convert_reduce_fusion = (f32[1536]{0:T(1024)}, bf16[2048,1536]{1,0:T(8,128)(2,1)}) fusion(f32[2048,1536]{1,0:T(8,128)} %get-tuple-element.280, bf16[1536,768]{1,0:T(8,128)(2,1)} %param.37, f32[2048,768]{1,0:T(8,128)} %get-tuple-element.275, f32[2048,1536]{1,0:T(8,128)} %get-tuple-element.289, f32[1536]{0:T(1024)S(1)} %convert_element_type.131), kind=kOutput, calls=%fused_computation.71 | convolution fusion | flops 4886886912 | bytes 40120320 | tf_op jit(solution)/shard_map/dot_general | solution.py:23
  250.6 9.7 %fusion.85 = f32[2048,768]{1,0:T(8,128)} fusion(bf16[2048,1536]{1,0:T(8,128)(2,1)} %get-tuple-element.291, bf16[768,1536]{1,0:T(8,128)(2,1)S(1)} %copy-done), kind=kOutput, calls=%fused_computation.149 | convolution fusion | flops 4831838208 | bytes 14942208 | tf_op jit(solution)/shard_map/dot_general | solution.py:23
  260.3 33.3 %all-reduce.12.cloned.1.call-done = f32[2048,768]{1,0:T(8,128)} async-done(((f32[2048,768]{1,0:T(8,128)}), f32[2048,768]{1,0:T(8,128)}) %all-reduce.12.cloned.1.call-update) | async-done | bytes 6291472 | tf_op jit(solution)/shard_map/psum | solution.py:259
  293.6 8.4 multiply_reduce_fusion.2
  302.1 5.5 subtract_multiply_fusion
  322.3 70.3 %while.27 = (s32[]{:T(128)}, bf16[4,512,6,64]{1,3,2,0:T(8,128)(2,1)}, bf16[4,512,6,64]{1,3,2,0:T(8,128)(2,1)}, bf16[4,512,6,64]{1,3,2,0:T(8,128)(2,1)}, bf16[4,5...) while((s32[]{:T(128)}, ...), condition=%wide.region_17.18_spmd, body=%wide.region_15.17_spmd.sunk | while | flops 1031730688 | bytes 52267136 | solution.py:174
  409.1 11.1 %all-reduce.16.cloned.1.call-start = ((), (), s32[]{:S(2)}) async-start(), calls=%async_computation.4 | async-start | bytes 28311552 | tf_op jit(solution)/shard_map/psum | solution.py:275
  420.2 12.6 %fusion.76 = f32[768,1536]{1,0:T(8,128)} fusion(bf16[2048,1536]{1,0:T(8,128)(2,1)} %get-tuple-element.291, f32[2048,768]{1,0:T(8,128)} %copy-done.2, f32[768]{0:T(1024)S(1)} %copy-done.30, f32[768]{0:T(1024)S(1)} %convert_element_type.128, f32[2048]{0:T(1024)S(1)} %add_rsqrt_fusion.1, f32[2048]{0:T(1024)S(1)} %broadcast_multiply_fusion.5), kind=kOutput, calls=%fused_computation.143 | convolution fusion | flops 4839702528 | bytes 17324032 | tf_op jit(solution)/shard_map/dot_general | solution.py:17
  432.8 10.6 %fusion.73 = f32[1536,768]{1,0:T(8,128)} fusion(bf16[2048,1536]{1,0:T(8,128)(2,1)} %copy-done.42, f32[2048,768]{1,0:T(8,128)} %get-tuple-element.275), kind=kOutput, calls=%fused_computation.123 | convolution fusion | flops 4833411072 | bytes 17301504 | tf_op jit(solution)/shard_map/dot_general | solution.py:17
  450.7 5.2 fusion.70
  459.6 6.1 multiply_reduce_fusion.1
  469.7 81.9 %all-reduce = (f32[384]{0:T(512)}, f32[384]{0:T(512)}, f32[768]{0:T(1024)}, f32[768]{0:T(1024)}, f32[768]{0:T(1024)}, /*index=5*/f32[1536]{0:T(1024)}, f32[768]{...) all-reduce(f32[384]{0:T(512)S(1)} %reduce_sum.265, ...), channel_id=1, replica_groups=mesh['wide'=16,'narrow'=2] {'wide'}, use_global_device_ids=true, to_apply=%region_23.24 | all-reduce | flops 6917 | bytes 55336 | tf_op jit(solution)/shard_map/psum | solution.py:275
  553.3 304.8 %all-reduce.16.cloned.1.call-done = (f32[768,384]{0,1:T(8,128)}, f32[768,384]{0,1:T(8,128)}, f32[768,384]{0,1:T(8,128)}, f32[384,768]{1,0:T(8,128)}, f32[768,1536]{1,0:T(8,128)}, /*index=5*/f32[1536,768]{1,0:T(8,128)}) async-done(((f32[768,384]{0,1:T(8,128)}, f32[768,384]{0,1:T(8,128)}, f32[768,384]{0,1:T(8,128)}, f32[384,768]{1,0:T(8,128)}, f32[768,1536]{1,0:T(8,128)}, /*index=5*/f32[1536,768]{1,0:T(8,128)}), ...) | async-done | bytes 14155792 | tf_op jit(solution)/shard_map/psum | solution.py:275
  867.2 5.5 copy.120
  (238 shorter events, 215.0 us)
Async XLA Ops:
  7.2 127.4 %copy-start = (bf16[768,1536]{1,0:T(8,128)(2,1)S(1)}, bf16[768,1536]{1,0:T(8,128)(2,1)}, u32[]{:S(2)}) copy-start(bf16[768,1536]{1,0:T(8,128)(2,1)} %param.35) | copy-start | bytes 7077892
  7.2 121.9 %all-reduce.8.cloned.1.call-start = ((), (), s32[]{:S(2)}) async-start(), calls=%async_computation | async-start | bytes 12582912 | tf_op jit(solution)/shard_map/psum | solution.py:253
  13.0 9.4 %copy-start.40 = (bf16[384]{0:T(512)(128)(2,1)S(1)}, bf16[384]{0:T(512)(128)(2,1)}, u32[]{:S(2)}) copy-start(bf16[384]{0:T(512)(128)(2,1)} %param.29) | copy-start | bytes 2308
  13.1 9.4 %copy-start.15 = (bf16[768,384]{1,0:T(8,128)(2,1)S(1)}, bf16[768,384]{1,0:T(8,128)(2,1)}, u32[]{:S(2)}) copy-start(bf16[768,384]{1,0:T(8,128)(2,1)} %param.26) | copy-start | bytes 1769476
  27.3 9.4 %copy-start.17 = (bf16[768,384]{1,0:T(8,128)(2,1)S(1)}, bf16[768,384]{1,0:T(8,128)(2,1)}, u32[]{:S(2)}) copy-start(bf16[768,384]{1,0:T(8,128)(2,1)} %param.27) | copy-start | bytes 1769476
  41.5 9.3 %copy-start.31 = (s32[2048]{0:T(1024)S(1)}, s32[2048]{0:T(1024)}, u32[]{:S(2)}) copy-start(s32[2048]{0:T(1024)} %param.24) | copy-start | bytes 24580
  41.5 9.4 %copy-start.22 = (s32[2048]{0:T(1024)S(1)}, s32[2048]{0:T(1024)}, u32[]{:S(2)}) copy-start(s32[2048]{0:T(1024)} %param.25) | copy-start | bytes 24580
  85.3 8.8 %copy-start.20 = (s32[4,512]{1,0:T(4,128)}, s32[4,512]{1,0:T(4,128)S(1)}, u32[]{:S(2)}) copy-start(s32[4,512]{1,0:T(4,128)S(1)} %get-tuple-element.544) | copy-start | bytes 24580
  85.4 8.8 %copy-start.21 = (s32[4,512]{1,0:T(4,128)}, s32[4,512]{1,0:T(4,128)S(1)}, u32[]{:S(2)}) copy-start(s32[4,512]{1,0:T(4,128)S(1)} %get-tuple-element.545) | copy-start | bytes 24580
  94.2 117.4 %all-reduce.10.cloned.1.call-start = ((), (), s32[]{:S(2)}) async-start(), calls=%async_computation.1 | async-start | bytes 12582912 | tf_op jit(solution)/shard_map/psum | solution.py:256
  94.3 117.2 %copy-start.29 = (f32[768]{0:T(1024)}, f32[768]{0:T(1024)S(1)}, u32[]{:S(2)}) copy-start(f32[768]{0:T(1024)S(1)} %convert_element_type.129) | copy-start | bytes 9220
  133.7 35.0 %copy-start.2 = (f32[2048,768]{1,0:T(8,128)}, f32[2048,768]{1,0:T(8,128)S(1)}, u32[]{:S(2)}) copy-start(f32[2048,768]{1,0:T(8,128)S(1)} %get-tuple-element.282) | copy-start | bytes 18874372
  134.6 36.8 %copy-start.41 = (bf16[1536,768]{1,0:T(8,128)(2,1)S(1)}, bf16[1536,768]{1,0:T(8,128)(2,1)}, u32[]{:S(2)}) copy-start(bf16[1536,768]{1,0:T(8,128)(2,1)} %param.37) | copy-start | bytes 7077892
  178.2 115.4 %all-reduce.12.cloned.1.call-start = ((), (), s32[]{:S(2)}) async-start(), calls=%async_computation.2 | async-start | bytes 12582912 | tf_op jit(solution)/shard_map/psum | solution.py:259
  260.3 199.3 %all-reduce.14.cloned.1.call-start = ((), (), s32[]{:S(2)}) async-start(), calls=%async_computation.3 | async-start | bytes 6291456 | tf_op jit(solution)/shard_map/psum | solution.py:262
  313.0 9.3 %copy-start.3 = (bf16[4,512,6,64]{1,3,2,0:T(8,128)(2,1)S(1)}, bf16[4,512,6,64]{1,3,2,0:T(8,128)(2,1)}, u32[]{:S(2)}) copy-start(bf16[4,512,6,64]{1,3,2,0:T(8,128)(2,1)} %get-tuple-element.515) | copy-start | bytes 4718596
  405.4 14.8 %copy-start.30 = (f32[768]{0:T(1024)S(1)}, f32[768]{0:T(1024)}, u32[]{:S(2)}) copy-start(f32[768]{0:T(1024)} %copy-done.29) | copy-start | bytes 9220
  409.1 449.0 %all-reduce.16.cloned.1.call-start = ((), (), s32[]{:S(2)}) async-start(), calls=%async_computation.4 | async-start | bytes 28311552 | tf_op jit(solution)/shard_map/psum | solution.py:275
  432.8 10.6 %copy-start.9 = (bf16[48,8,4,512]{3,1,2,0:T(8,128)(2,1)S(1)}, bf16[48,8,4,512]{3,1,2,0:T(8,128)(2,1)}, u32[]{:S(2)}) copy-start(bf16[48,8,4,512]{3,1,2,0:T(8,128)(2,1)} %copy-done.8) | copy-start | bytes 4718596
  432.8 10.6 %copy-start.11 = (bf16[2048,768]{1,0:T(8,128)(2,1)S(1)}, bf16[2048,768]{1,0:T(8,128)(2,1)}, u32[]{:S(2)}) copy-start(bf16[2048,768]{1,0:T(8,128)(2,1)} %param.23) | copy-start | bytes 9437188
  459.5 10.1 %copy-start.26 = (f32[768]{0:T(1024)S(1)}, f32[768]{0:T(1024)}, u32[]{:S(2)}) copy-start(f32[768]{0:T(1024)} %get-tuple-element.201) | copy-start | bytes 9220
  459.5 10.1 %copy-start.27 = (f32[768]{0:T(1024)S(1)}, f32[768]{0:T(1024)}, u32[]{:S(2)}) copy-start(f32[768]{0:T(1024)} %get-tuple-element.215) | copy-start | bytes 9220
  459.5 10.1 %copy-start.28 = (f32[768]{0:T(1024)S(1)}, f32[768]{0:T(1024)}, u32[]{:S(2)}) copy-start(f32[768]{0:T(1024)} %get-tuple-element.213) | copy-start | bytes 9220
  459.5 10.1 %copy-start.32 = (f32[1536]{0:T(1024)S(1)}, f32[1536]{0:T(1024)}, u32[]{:S(2)}) copy-start(f32[1536]{0:T(1024)} %get-tuple-element.290) | copy-start | bytes 18436
  (26 other events, 99.2 us)
Sparse Core Ops, SparseCore 0:
  94.3 34.7 all-reduce.7
  178.4 33.1 all-reduce.9
  260.4 33.1 all-reduce.11
  409.2 24.3 all-reduce.13
  456.1 401.9 all-reduce.15
where the time goes:
time: 887 us; the launch traced here: 882 us
  waiting for transfers between devices  406 us (46%)
  matrix products  214 us (24%)
  local copies, waits for them, and re-layouts  85.2 us (10%)
  blocking collectives  81.9 us (9%)
  other arithmetic  67.5 us (8%)
  between operations  15.1 us (2%)
  starting transfers between devices  11.3 us (1%)
    psum x1, waiting for transfers between devices, body(): summed = lax.psum(sharded + replicated + extra_members, 'wide')  305 us
    psum x1, blocking collectives, body(): summed = lax.psum(sharded + replicated + extra_members, 'wide')  81.9 us
    dot_general x6, matrix products, right_contract(): lax.dot_general(left, right, (((1,), (1,)), ((), ())), preferred_element_...  42 us
    dot_general x6, matrix products, left_contract(): lax.dot_general(left, right, (((0,), (0,)), ((), ())), preferred_element_...  35.7 us
    psum x1, waiting for transfers between devices, sum_attn(): return lax.psum(values, 'narrow')  34.7 us
    dot_general x1, matrix products, run_layer(): jnp.dot(first_low, w_ffn_in, preferred_element_type=f32)  34.1 us
    psum x1, waiting for transfers between devices, sum_hidden(): return lax.psum(values, 'narrow')  33.3 us
    psum x1, waiting for transfers between devices, sum_ffn(): return lax.psum(values, 'narrow')  32.6 us
  transfers between devices with their start and end apart: 5, of which 4 were waited for; matrix products, arithmetic and copies ran while one was open for 6% of the time, Pallas kernels for 0%

commit v1 on v0

v1 whole, which is shorter than its diff:
```python
from functools import partial

import jax
import jax.numpy as jnp
from jax import lax
from jax.sharding import PartitionSpec as P

D = 768
HEAD_DIM = 64
SEQ_LEN = 512
norm_eps = 1e-06
f32 = jnp.float32
bf16 = jnp.bfloat16


def left_contract(left, right):
    return lax.dot_general(
        left, right, (((0,), (0,)), ((), ())), preferred_element_type=f32
    )


def right_contract(left, right):
    return lax.dot_general(
        left, right, (((1,), (1,)), ((), ())), preferred_element_type=f32
    )


def layer_norm(values, gain, shift):
    centred = values - jnp.mean(values, axis=-1, keepdims=True)
    inverse = lax.rsqrt(jnp.mean(centred * centred, axis=-1, keepdims=True) + norm_eps)
    normed = centred * inverse
    return (normed * gain + shift, normed, inverse)


def norm_back(grad_rows, normed, inverse, gain):
    inner = grad_rows * gain
    centre_part = jnp.mean(inner, axis=-1, keepdims=True)
    slope_part = jnp.mean(inner * normed, axis=-1, keepdims=True)
    return inverse * (inner - centre_part - normed * slope_part)


def masked_scores(queries, key_rows, seg_row, valid_row, scale):
    scores = (
        jnp.einsum("qhd,khd->hqk", queries, key_rows, preferred_element_type=f32) * scale
    )
    allowed = (seg_row[:, None] == seg_row[None, :]) & (valid_row[None, :] == 1)
    return jnp.where(allowed[None], scores, -1e30)


def attend_forward(packed, scale):
    queries, key_rows, value_rows, seg_row, valid_row = packed
    scores = masked_scores(queries, key_rows, seg_row, valid_row, scale)
    peak = jnp.max(scores, axis=-1, keepdims=True)
    shifted = jnp.exp(scores - peak)
    totals = jnp.sum(shifted, axis=-1, keepdims=True)
    weights = (shifted / totals).astype(bf16)
    context = jnp.einsum("hqk,khd->qhd", weights, value_rows, preferred_element_type=f32)
    return (context.astype(bf16), peak + jnp.log(totals))


def attend_backward(packed, scale):
    queries, key_rows, value_rows, seg_row, valid_row, log_totals, grad_context = packed
    probs = jnp.exp(masked_scores(queries, key_rows, seg_row, valid_row, scale) - log_totals)
    grad_probs = jnp.einsum(
        "qhd,khd->hqk", grad_context, value_rows, preferred_element_type=f32
    )
    centred = grad_probs - jnp.sum(grad_probs * probs, axis=-1, keepdims=True)
    grad_scores = (probs * centred).astype(bf16)
    grad_queries = (
        jnp.einsum("hqk,khd->qhd", grad_scores, key_rows, preferred_element_type=f32) * scale
    )
    grad_keys = (
        jnp.einsum("hqk,qhd->khd", grad_scores, queries, preferred_element_type=f32) * scale
    )
    grad_values = jnp.einsum(
        "hqk,qhd->khd", probs.astype(bf16), grad_context, preferred_element_type=f32
    )
    return (grad_queries.astype(bf16), grad_keys.astype(bf16), grad_values.astype(bf16))


def swap_narrow(values):
    return lax.ppermute(values, "narrow", [(0, 1), (1, 0)])


def swap_wide(values, bit, size):
    return lax.ppermute(values, "wide", [(i, i ^ (1 << bit)) for i in range(size)])


def halve(values, orders, size):
    me = lax.axis_index("wide")
    states = list(values)
    for step in range(len(orders[0])):
        fresh = []
        for state, order in zip(states, orders):
            bit = order[step]
            half = state.shape[0] // 2
            mine = (me >> bit) & 1
            kept = lax.dynamic_slice_in_dim(state, mine * half, half, 0)
            sent = lax.dynamic_slice_in_dim(state, (1 - mine) * half, half, 0)
            got = swap_wide(sent, bit, size)
            fresh.append((kept.astype(f32) + got.astype(f32)).astype(bf16))
        states = fresh
    return states


def double(states, orders, size):
    me = lax.axis_index("wide")
    for step in reversed(range(len(orders[0]))):
        fresh = []
        for state, order in zip(states, orders):
            bit = order[step]
            mine = (me >> bit) & 1
            got = swap_wide(state, bit, size)
            fresh.append(
                jnp.where(
                    mine == 1,
                    jnp.concatenate([got, state], 0),
                    jnp.concatenate([state, got], 0),
                )
            )
        states = fresh
    return states


def sum_wide(values, size):
    bits = size.bit_length() - 1
    if size != 1 << bits or values.shape[0] % (6 * size):
        return lax.psum(values, "wide").astype(f32)
    first = list(range(bits))
    orders = [first]
    if bits >= 3:
        rest = list(range(3, bits))
        orders = [[0, 1, 2] + rest, [1, 2, 0] + rest, [2, 0, 1] + rest]
        sixth = values.shape[0] // 6
        parts = [values[: 3 * sixth], values[3 * sixth : 5 * sixth], values[5 * sixth :]]
    else:
        parts = [values]
    parts = double(halve(parts, orders, size), orders, size)
    return jnp.concatenate(parts, 0).astype(f32)


def sum_small(values, size):
    values = values + swap_narrow(values)
    bits = size.bit_length() - 1
    if size != 1 << bits:
        return lax.psum(values, "wide")
    for bit in range(bits):
        values = values + swap_wide(values, bit, size)
    return values


def body(size, *arrays):
    (
        inputs, segments, valid, w_query, w_key, w_value, b_query, b_value, w_attn_out, b_attn_out,
        gain_one, shift_one, w_ffn_in, b_ffn_in, w_ffn_out, b_ffn_out, gain_two, shift_two, out_grad,
    ) = arrays
    side = lax.axis_index("narrow")
    rows = inputs.shape[0] // 2
    head_width = w_query.shape[1]

    def mine(array):
        return lax.dynamic_slice_in_dim(array, side * rows, rows, 0)

    def both(array, axis):
        return jnp.concatenate([array, swap_narrow(array)], axis)

    def join_rows(array):
        other = swap_narrow(array)
        return jnp.where(
            side == 0,
            jnp.concatenate([array, other], 0),
            jnp.concatenate([other, array], 0),
        )

    hidden_in, seg_rows, valid_rows, cotangent = (mine(a) for a in (inputs, segments, valid, out_grad))
    w_query, w_key, w_value = (both(w, 1) for w in (w_query, w_key, w_value))
    b_query, b_value = both(b_query, 0), both(b_value, 0)
    w_attn_out = both(w_attn_out, 0)
    w_ffn_in, b_ffn_in, w_ffn_out = both(w_ffn_in, 1), both(b_ffn_in, 0), both(w_ffn_out, 0)

    seq_count = rows // SEQ_LEN
    heads = 2 * head_width // HEAD_DIM
    scale = HEAD_DIM ** (-0.5)

    def split_heads(array):
        return array.reshape(seq_count, SEQ_LEN, heads, HEAD_DIM)

    queries = (jnp.dot(hidden_in, w_query, preferred_element_type=f32) + b_query.astype(f32)).astype(bf16)
    key_rows = jnp.dot(hidden_in, w_key, preferred_element_type=f32).astype(bf16)
    value_rows = (jnp.dot(hidden_in, w_value, preferred_element_type=f32) + b_value.astype(f32)).astype(bf16)
    head_inputs = (
        split_heads(queries),
        split_heads(key_rows),
        split_heads(value_rows),
        seg_rows.reshape(seq_count, SEQ_LEN),
        valid_rows.reshape(seq_count, SEQ_LEN),
    )
    context, log_totals = lax.map(partial(attend_forward, scale=scale), head_inputs)
    context = context.reshape(rows, 2 * head_width)
    attn = jnp.dot(context, w_attn_out, preferred_element_type=f32) + b_attn_out.astype(f32)
    mixed = hidden_in.astype(f32) + attn
    first, normed_one, inverse_one = layer_norm(mixed, gain_one.astype(f32), shift_one.astype(f32))
    first_low = first.astype(bf16)
    pre_act = jnp.dot(first_low, w_ffn_in, preferred_element_type=f32) + b_ffn_in.astype(f32)
    activated = jax.nn.gelu(pre_act, approximate=False).astype(bf16)
    ffn_out = jnp.dot(activated, w_ffn_out, preferred_element_type=f32) + b_ffn_out.astype(f32)
    second = first + ffn_out
    final, normed_two, inverse_two = layer_norm(second, gain_two.astype(f32), shift_two.astype(f32))
    output = join_rows(final.astype(bf16))
    valid_float = valid_rows.astype(f32)
    grad_out = cotangent.astype(f32) * valid_float[:, None]
    d_gain_two = jnp.sum(grad_out * normed_two, axis=0)
    d_shift_two = jnp.sum(grad_out, axis=0)
    grad_second = norm_back(grad_out, normed_two, inverse_two, gain_two.astype(f32))
    d_b_ffn_out = jnp.sum(grad_second, axis=0)
    low_second = grad_second.astype(bf16)

    def reduce_rows(left, right):
        half = left.shape[1] // 2
        sent = left_contract(left[:, half:], right).astype(bf16)
        kept = left_contract(left[:, :half], right)
        return sum_wide((kept + swap_narrow(sent).astype(f32)).astype(bf16), size)

    def reduce_columns(left, kept_right, sent_right):
        sent = left_contract(left, sent_right).astype(bf16)
        kept = left_contract(left, kept_right)
        return sum_wide((kept + swap_narrow(sent).astype(f32)).astype(bf16), size)

    d_w_ffn_out = reduce_rows(activated, low_second)
    grad_act = right_contract(low_second, w_ffn_out)
    unused_value, gelu_back = jax.vjp(partial(jax.nn.gelu, approximate=False), pre_act)
    grad_pre = gelu_back(grad_act)[0].astype(bf16)
    d_b_ffn_in = jnp.sum(grad_pre.astype(f32), axis=0)
    half = grad_pre.shape[1] // 2
    d_w_ffn_in = reduce_columns(first_low, grad_pre[:, :half], grad_pre[:, half:])
    grad_first = grad_second + right_contract(grad_pre, w_ffn_in)
    d_gain_one = jnp.sum(grad_first * normed_one, axis=0)
    d_shift_one = jnp.sum(grad_first, axis=0)
    grad_mixed = norm_back(grad_first, normed_one, inverse_one, gain_one.astype(f32))
    d_b_attn_out = jnp.sum(grad_mixed, axis=0)
    low_mixed = grad_mixed.astype(bf16)
    d_w_attn_out = reduce_rows(context, low_mixed)
    grad_context = right_contract(low_mixed, w_attn_out).astype(bf16)
    back_inputs = head_inputs + (log_totals, split_heads(grad_context))
    grads = lax.map(partial(attend_backward, scale=scale), back_inputs)
    grad_queries, grad_keys, grad_values = (g.reshape(rows, 2 * head_width) for g in grads)
    d_b_query = jnp.sum(grad_queries.astype(f32), axis=0)
    d_b_value = jnp.sum(grad_values.astype(f32), axis=0)
    three = (grad_queries, grad_keys, grad_values)
    d_w_three = reduce_columns(
        hidden_in,
        jnp.concatenate([g[:, :head_width] for g in three], 1),
        jnp.concatenate([g[:, head_width:] for g in three], 1),
    )
    grad_in = (
        grad_mixed
        + right_contract(grad_queries, w_query)
        + right_contract(grad_keys, w_key)
        + right_contract(grad_values, w_value)
    )
    input_grad = join_rows(grad_in.astype(bf16))
    stats = jnp.stack(
        [
            jnp.sum(valid_float * jnp.sum(g * g, axis=-1))
            for g in (grad_in, grad_second, grad_first, grad_mixed)
        ]
        + [jnp.sum(valid_float)]
    )

    def by_side(array):
        half = array.shape[0] // 2
        return jnp.where(side == 0, array, jnp.roll(array, half))

    small = sum_small(
        jnp.concatenate(
            [by_side(d_b_query), by_side(d_b_value), by_side(d_b_ffn_in)]
            + [d_b_attn_out, d_gain_one, d_shift_one, d_b_ffn_out, d_gain_two, d_shift_two]
            + [jnp.pad(stats, (0, 128 - 5))]
        ),
        size,
    )
    ends = []
    at = 0
    for length in (2 * head_width, 2 * head_width, b_ffn_in.shape[0]) + (D,) * 6 + (128,):
        ends.append(small[at : at + length])
        at += length

    def own(array):
        half = array.shape[0] // 2
        return lax.dynamic_slice_in_dim(array, side * half, half, 0)

    rms = jnp.sqrt(ends[9][:4] / (ends[9][4] * D))
    return (
        output,
        input_grad,
        d_w_three[:, :head_width],
        d_w_three[:, head_width : 2 * head_width],
        d_w_three[:, 2 * head_width :],
        own(ends[0]),
        own(ends[1]),
        d_w_attn_out,
        ends[3],
        ends[4],
        ends[5],
        d_w_ffn_in,
        own(ends[2]),
        d_w_ffn_out,
        ends[6],
        ends[7],
        ends[8],
        rms,
    )


def solution(mesh):
    row, col = P("narrow", None), P(None, "narrow")
    one, rows = P("narrow"), P("wide", None)
    in_specs = (
        rows, P("wide"), P("wide"), col, col, col, one, one, row, P(), P(), P(), col, one, row, P(), P(), P(), rows,
    )
    out_specs = (
        rows, rows, col, col, col, one, one, row, P(), P(), P(), col, one, row, P(), P(), P(), P(),
    )
    return jax.shard_map(
        partial(body, mesh.shape["wide"]), mesh=mesh, in_specs=in_specs, out_specs=out_specs, check_vma=False
    )
```

time: 887 us -> 685 us (0.77)
  waiting for transfers between devices: 406 us -> 230 us
  starting transfers between devices: 11.3 us -> 113 us
  blocking collectives: 81.9 us -> 0 us
  matrix products: 214 us -> 173 us
  local copies, waits for them, and re-layouts: 85.2 us -> 101 us
  other arithmetic: 67.5 us -> 54.6 us
  between operations: 15.1 us -> 4 us
    psum x5 -> x0, waiting for transfers between devices: 405 us -> none  [the longest x1 305 us: body(): summed = lax.psum(sharded + replicated + extra_members, 'wide')]
    ppermute x0 -> x116, waiting for transfers between devices: none -> 230 us  [the longest x100 228 us: swap_wide(): lax.ppermute(values, 'wide', [(i, i ^ 1 << bit) for i in range(size)])]
    ppermute x0 -> x116, starting transfers between devices: none -> 113 us  [the longest x100 109 us: swap_wide(): lax.ppermute(values, 'wide', [(i, i ^ 1 << bit) for i in range(size)])]
    psum x1 -> x0, blocking collectives: 81.9 us -> none  [body(): summed = lax.psum(sharded + replicated + extra_members, 'wide')]
    dot_general x26 -> x16, matrix products: 114 us -> 81.6 us  [the longest x1 37 us: body(): jnp.dot(first_low, w_ffn_in, preferred_element_type=f32)]
    reduce_sum x9 -> x6, other arithmetic: 38.5 us -> 12.7 us  [the longest x2 8.06 us: body(): jnp.sum(g * g, axis=-1)]
    convert_element_type x14 -> x65, other arithmetic: 8.65 us -> 27.4 us  [the longest x2 14.2 us: attend_backward(): grad_scores = (probs * centred).astype(bf16)]
    concatenate x0 -> x7, local copies, waits for them, and re-layouts: none -> 11.7 us  [the longest x6 11.7 us: both(): return jnp.concatenate([array, swap_narrow(array)], axis)]
  transfers between devices with their start and end apart: 5 -> 116, of which waited for: 4 -> 69; matrix products, arithmetic and copies ran while one was open for 6% -> 24% of each run, Pallas kernels for 0% -> 0%
where the time goes in v1:
time: 685 us; the launch traced here: 677 us
  waiting for transfers between devices  230 us (34%)
  matrix products  173 us (25%)
  starting transfers between devices  113 us (16%)
  local copies, waits for them, and re-layouts  101 us (15%)
  other arithmetic  54.6 us (8%)
    ppermute x100, waiting for transfers between devices, swap_wide(): lax.ppermute(values, 'wide', [(i, i ^ 1 << bit) for i in range(size)])  228 us
    ppermute x100, starting transfers between devices, swap_wide(): lax.ppermute(values, 'wide', [(i, i ^ 1 << bit) for i in range(size)])  109 us
    dot_general x6, matrix products, right_contract(): lax.dot_general(left, right, (((1,), (1,)), ((), ())), preferred_element_...  45.4 us
    dot_general x1, matrix products, body(): jnp.dot(first_low, w_ffn_in, preferred_element_type=f32)  37 us
    unnamed x201, local copies, waits for them, and re-layouts  36.6 us
    dot_general x8, matrix products, left_contract(): lax.dot_general(left, right, (((0,), (0,)), ((), ())), preferred_element_...  30.2 us
    convert_element_type x2, other arithmetic, attend_backward(): grad_scores = (probs * centred).astype(bf16)  14.2 us
  transfers between devices with their start and end apart: 116, of which 69 were waited for; matrix products, arithmetic and copies ran while one was open for 24% of the time, Pallas kernels for 0%

profile of v1, /device:TPU:0, one launch (start us, length us, event | category | flops | bytes accessed | tf_op | source)
XLA Modules:
  0.0 677.1 jit_solution(7718784344282976627)
XLA Ops:
  54.4 21.1 %while.26 = (s32[]{:T(128)}, bf16[2,512,12,64]{1,3,2,0:T(8,128)(2,1)}, f32[2,12,512,1]{2,1,3,0:T(8,128)S(1)}, bf16[2,512,12,64]{1,3,2,0:T(8,128)(2,1)}, s32[2,51...) while((s32[]{:T(128)}, ...), condition=%wide.region_3.4_spmd, body=%wide.region_0.3_spmd.sunk | while | flops 843966976 | bytes 42175592 | solution.py:198
  59.5 5.5 fusion.167
  70.0 5.5 fusion.167
  87.9 37.0 %multiply_convert_fusion.3 = (bf16[1024,3072]{1,0:T(8,128)(2,1)S(1)}, f32[1024,3072]{1,0:T(8,128)}, f32[1024,3072]{1,0:T(8,128)}) fusion(f32[3072]{0:T(1024)S(1)} %copy-done.74, bf16[1024,768]{0,1:T(8,128)(2,1)S(1)} %fusion.76, bf16[768,3072]{1,0:T(8,128)(2,1)S(1)} %constant_dynamic-update-slice_fusion.8), kind=kOutput, calls=%fused_computation.71 | convolution fusion | flops 5039456256 | bytes 37761024 | tf_op jit(solution)/shard_map/dot_general | solution.py:204
  128.6 5.9 fusion.117
  142.2 19.6 %convert_reduce_fusion = (f32[3072]{0:T(1024)}, bf16[1024,3072]{1,0:T(8,128)(2,1)}) fusion(f32[1024,3072]{1,0:T(8,128)} %get-tuple-element.265, bf16[3072,768]{1,0:T(8,128)(2,1)} %copy-done.42, f32[1024,768]{0,1:T(8,128)} %get-tuple-element.260, f32[1024,3072]{1,0:T(8,128)} %get-tuple-element.296, f32[3072]{0:T(1024)S(1)} %copy-done.74), kind=kOutput, calls=%fused_computation.69 | convolution fusion | flops 4886098944 | bytes 39346176 | tf_op jit(solution)/shard_map/dot_general | solution.py:23
  161.8 10.8 %multiply_reduce_fusion.2 = (f32[1024]{0:T(1024)}, f32[768]{0:T(1024)}, f32[1024]{0:T(1024)S(1)}, f32[1024]{0:T(1024)S(1)}, f32[768]{0:T(1024)}, /*index=5*/f32[1024,768]{0,1:T(8,128)S(1)}) fusion(f32[768]{0:T(1024)S(1)} %copy-done.61, f32[1024]{0:T(1024)S(1)} %add_rsqrt_fusion.1, f32[1024,768]{0,1:T(8,128)S(1)} %get-tuple-element.295, ...), kind=kOutput, calls=%fused_computation.100 | convolution fusion | flops 4841270272 | bytes 20476928 | tf_op jit(solution)/shard_map/dot_general | solution.py:23
  190.1 49.1 %while.27 = (s32[]{:T(128)}, bf16[2,512,12,64]{1,3,2,0:T(8,128)(2,1)}, bf16[2,512,12,64]{1,3,2,0:T(8,128)(2,1)}, bf16[2,512,12,64]{1,3,2,0:T(8,128)(2,1)}, bf16[...) while((s32[]{:T(128)}, ...), condition=%wide.region_14.15_spmd, body=%wide.region_12.14_spmd.sunk | while | flops 2062936576 | bytes 141236528 | solution.py:245
  192.7 6.8 %multiply_reduce_fusion.17 = (f32[12,512]{1,0:T(8,128)S(1)}, f32[12,512,512]{1,2,0:T(8,128)}) fusion(f32[12,512,512]{1,2,0:T(8,128)S(1)} %fusion.176, f32[12,512]{1,0:T(8,128)S(1)} %dynamic-slice_bitcast_fusion.2, pred[512,512]{0,1:T(8,128)(4,1)S(1)} %compare_and_fusion.5, bf16[2,512,12,64]{1,3,2,0:T(8,128)(2,1)S(1)} %copy-done.9, ...), kind=kOutput, calls=%fused_computation.25.clone.1 | convolution fusion | flops 418375680 | bytes 27059200 | tf_op jit(solution)/shard_map/while/body/eval_jaxpr/qhd,khd->hqk/dot_general | solution.py:64
  199.5 7.1 %multiply_convert_fusion.5 = bf16[12,512,512]{1,2,0:T(8,128)(2,1)S(1)} fusion(f32[12,512,512]{1,2,0:T(8,128)} %get-tuple-element.428, f32[12,512,512]{1,2,0:T(8,128)S(1)} %fusion.176, f32[12,512]{1,0:T(8,128)S(1)} %get-tuple-element.429, f32[12,512]{1,0:T(8,128)S(1)} %dynamic-slice_bitcast_fusion.2, pred[512,512]{0,1:T(8,128)(4,1)S(1)} %compare_and_fusion.5), kind=kLoop, calls=%fused_computation.24.clone.1 | loop fusion | flops 18874368 | bytes 31768576 | tf_op jit(solution)/shard_map/while/body/eval_jaxpr/convert_element_type | solution.py:68
  217.1 6.8 %multiply_reduce_fusion.17 = (f32[12,512]{1,0:T(8,128)S(1)}, f32[12,512,512]{1,2,0:T(8,128)}) fusion(f32[12,512,512]{1,2,0:T(8,128)S(1)} %fusion.176, f32[12,512]{1,0:T(8,128)S(1)} %dynamic-slice_bitcast_fusion.2, pred[512,512]{0,1:T(8,128)(4,1)S(1)} %compare_and_fusion.5, bf16[2,512,12,64]{1,3,2,0:T(8,128)(2,1)S(1)} %copy-done.9, ...), kind=kOutput, calls=%fused_computation.25.clone.1 | convolution fusion | flops 418375680 | bytes 27059200 | tf_op jit(solution)/shard_map/while/body/eval_jaxpr/qhd,khd->hqk/dot_general | solution.py:64
  223.9 7.1 %multiply_convert_fusion.5 = bf16[12,512,512]{1,2,0:T(8,128)(2,1)S(1)} fusion(f32[12,512,512]{1,2,0:T(8,128)} %get-tuple-element.428, f32[12,512,512]{1,2,0:T(8,128)S(1)} %fusion.176, f32[12,512]{1,0:T(8,128)S(1)} %get-tuple-element.429, f32[12,512]{1,0:T(8,128)S(1)} %dynamic-slice_bitcast_fusion.2, pred[512,512]{0,1:T(8,128)(4,1)S(1)} %compare_and_fusion.5), kind=kLoop, calls=%fused_computation.24.clone.1 | loop fusion | flops 18874368 | bytes 31768576 | tf_op jit(solution)/shard_map/while/body/eval_jaxpr/convert_element_type | solution.py:68
  248.7 7.1 %convolution_convert_fusion = bf16[1536,768]{1,0:T(8,128)(2,1)} fusion(bf16[1024,3072]{1,0:T(8,128)(2,1)} %copy-done.89, f32[1024,768]{0,1:T(8,128)} %get-tuple-element.260), kind=kOutput, calls=%fused_computation.88 | convolution fusion | flops 2417885184 | bytes 8650752 | tf_op jit(solution)/shard_map/dot_general | solution.py:17
  255.8 5.8 convolution_convert_fusion.1
  274.8 6.3 multiply_reduce_fusion.4
  426.9 4.6 copy.83
  463.4 5.5 add_convert_fusion.1
  480.9 15.9 %collective-permute-done.25 = bf16[32,1152]{1,0:T(8,128)(2,1)S(1)} collective-permute-done((bf16[32,1152]{1,0:T(8,128)(2,1)S(1)}, bf16[32,1152]{1,0:T(8,128)(2,1)S(1)}, u32[]{:S(2)}, u32[]{:S(2)}) %collective-permute-start.25) | collective-permute-done | bytes 73760 | tf_op jit(solution)/shard_map/ppermute | solution.py:86
  502.6 6.2 collective-permute-done.83
  515.4 5.1 collective-permute-done.26
  580.4 4.8 collective-permute-done.89
  603.8 5.3 collective-permute-done.78
  609.2 5.3 collective-permute-done.103
  657.7 5.8 collective-permute-done.73
  (743 shorter events, 482.4 us)
Async XLA Ops:
  0.7 26.6 %collective-permute-start = (bf16[768,384]{1,0:T(8,128)(2,1)}, bf16[768,384]{1,0:T(8,128)(2,1)}, u32[]{:S(2)}, u32[]{:S(2)}) collective-permute-start(bf16[768,384]{1,0:T(8,128)(2,1)} %param.28), channel_id=1, source_target_pairs={{0,1},{1,0},{2,3},{3,2},{4,5},{5,4},{6,7},{7,6},{8,9},{9,8},{10,11... | collective-permute-start | bytes 1769480 | tf_op jit(solution)/shard_map/ppermute | solution.py:82
  1.2 23.0 %collective-permute-start.1 = (bf16[384]{0:T(512)(128)(2,1)}, bf16[384]{0:T(512)(128)(2,1)S(1)}, u32[]{:S(2)}, u32[]{:S(2)}) collective-permute-start(bf16[384]{0:T(512)(128)(2,1)} %param.30), channel_id=1, source_target_pairs={{0,1},{1,0},{2,3},{3,2},{4,5},{5,4},{6,7},{7,6},{8,9},{9,8},{10,11... | collective-permute-start | bytes 2312 | tf_op jit(solution)/shard_map/ppermute | solution.py:82
  1.3 34.5 %collective-permute-start.2 = (bf16[768,384]{1,0:T(8,128)(2,1)}, bf16[768,384]{1,0:T(8,128)(2,1)}, u32[]{:S(2)}, u32[]{:S(2)}) collective-permute-start(bf16[768,384]{1,0:T(8,128)(2,1)} %param.26), channel_id=1, source_target_pairs={{0,1},{1,0},{2,3},{3,2},{4,5},{5,4},{6,7},{7,6},{8,9},{9,8},{10,11... | collective-permute-start | bytes 1769480 | tf_op jit(solution)/shard_map/ppermute | solution.py:82
  1.7 39.9 %collective-permute-start.4 = (bf16[768,384]{1,0:T(8,128)(2,1)}, bf16[768,384]{1,0:T(8,128)(2,1)}, u32[]{:S(2)}, u32[]{:S(2)}) collective-permute-start(bf16[768,384]{1,0:T(8,128)(2,1)} %param.27), channel_id=1, source_target_pairs={{0,1},{1,0},{2,3},{3,2},{4,5},{5,4},{6,7},{7,6},{8,9},{9,8},{10,11... | collective-permute-start | bytes 1769480 | tf_op jit(solution)/shard_map/ppermute | solution.py:82
  1.8 78.4 %collective-permute-start.5 = (bf16[384,768]{1,0:T(8,128)(2,1)}, bf16[384,768]{1,0:T(8,128)(2,1)}, u32[]{:S(2)}, u32[]{:S(2)}) collective-permute-start(bf16[384,768]{1,0:T(8,128)(2,1)} %param.31), channel_id=1, source_target_pairs={{0,1},{1,0},{2,3},{3,2},{4,5},{5,4},{6,7},{7,6},{8,9},{9,8},{10,11... | collective-permute-start | bytes 1769480 | tf_op jit(solution)/shard_map/ppermute | solution.py:82
  26.5 58.2 %collective-permute-start.6 = (bf16[768,1536]{1,0:T(8,128)(2,1)}, bf16[768,1536]{1,0:T(8,128)(2,1)}, u32[]{:S(2)}, u32[]{:S(2)}) collective-permute-start(bf16[768,1536]{1,0:T(8,128)(2,1)} %param.35), channel_id=1, source_target_pairs={{0,1},{1,0},{2,3},{3,2},{4,5},{5,4},{6,7},{7,6},{8,9},{9,8},{10,11... | collective-permute-start | bytes 7077896 | tf_op jit(solution)/shard_map/ppermute | solution.py:82
  27.3 97.7 %collective-permute-start.8 = (bf16[1536,768]{1,0:T(8,128)(2,1)}, bf16[1536,768]{1,0:T(8,128)(2,1)}, u32[]{:S(2)}, u32[]{:S(2)}) collective-permute-start(bf16[1536,768]{1,0:T(8,128)(2,1)} %param.37), channel_id=1, source_target_pairs={{0,1},{1,0},{2,3},{3,2},{4,5},{5,4},{6,7},{7,6},{8,9},{9,8},{10,11... | collective-permute-start | bytes 7077896 | tf_op jit(solution)/shard_map/ppermute | solution.py:82
  298.9 164.4 %collective-permute-start.91 = (bf16[1536,768]{1,0:T(8,128)(2,1)}, bf16[1536,768]{1,0:T(8,128)(2,1)}, u32[]{:S(2)}, u32[]{:S(2)}) collective-permute-start(bf16[1536,768]{1,0:T(8,128)(2,1)} %convolution_convert_fusion), channel_id=1, source_target_pairs={{0,1},{1,0},{2,3},{3,2},{4,5},{5,4},{6,7},{7,6},{8,9},{9,8},{10,11... | collective-permute-start | bytes 7077896 | tf_op jit(solution)/shard_map/ppermute | solution.py:82
  299.0 170.1 %collective-permute-start.66 = (bf16[768,1536]{1,0:T(8,128)(2,1)}, bf16[768,1536]{1,0:T(8,128)(2,1)}, u32[]{:S(2)}, u32[]{:S(2)}) collective-permute-start(bf16[768,1536]{1,0:T(8,128)(2,1)} %convolution_convert_fusion.1), channel_id=1, source_target_pairs={{0,1},{1,0},{2,3},{3,2},{4,5},{5,4},{6,7},{7,6},{8,9},{9,8},{10,11... | collective-permute-start | bytes 7077896 | tf_op jit(solution)/shard_map/ppermute | solution.py:82
  308.6 95.7 %collective-permute-start.11 = (bf16[768,1152]{1,0:T(8,128)(2,1)S(1)}, bf16[768,1152]{1,0:T(8,128)(2,1)S(1)}, u32[]{:S(2)}, u32[]{:S(2)}) collective-permute-start(bf16[768,1152]{1,0:T(8,128)(2,1)S(1)} %convolution_convert_fusion.2), channel_id=1, source_target_pairs={{0,1},{1,0},{2,3},{3,2},{4,5},{5,4},{6,7},{7,6},{8,9},{9,8},{10,11... | collective-permute-start | bytes 5308424 | tf_op jit(solution)/shard_map/ppermute | solution.py:82
  308.7 109.1 %collective-permute-start.10 = (bf16[1024,768]{0,1:T(8,128)(2,1)S(1)}, bf16[1024,768]{0,1:T(8,128)(2,1)S(1)}, u32[]{:S(2)}, u32[]{:S(2)}) collective-permute-start(bf16[1024,768]{0,1:T(8,128)(2,1)S(1)} %copy-done.16), channel_id=1, source_target_pairs={{0,1},{1,0},{2,3},{3,2},{4,5},{5,4},{6,7},{7,6},{8,9},{9,8},{10,11... | collective-permute-start | bytes 4718600 | tf_op jit(solution)/shard_map/ppermute | solution.py:82
  458.3 21.7 %collective-permute-start.13 = (bf16[96,1152]{1,0:T(8,128)(2,1)S(1)}, bf16[96,1152]{1,0:T(8,128)(2,1)S(1)}, u32[]{:S(2)}, u32[]{:S(2)}) collective-permute-start(bf16[96,1152]{1,0:T(8,128)(2,1)S(1)} %constant_dynamic-slice_fusion.58), channel_id=1, source_target_pairs={{0,4},{2,6},{4,0},{6,2},{8,12},{10,14},{12,8},{14,10},{16,20},{18,... | collective-permute-start | bytes 663560 | tf_op jit(solution)/shard_map/ppermute | solution.py:86
  474.9 111.4 %collective-permute-start.92 = (bf16[384,768]{1,0:T(8,128)(2,1)S(1)}, bf16[384,768]{1,0:T(8,128)(2,1)S(1)}, u32[]{:S(2)}, u32[]{:S(2)}) collective-permute-start(bf16[384,768]{1,0:T(8,128)(2,1)S(1)} %constant_dynamic-slice_fusion.15), channel_id=1, source_target_pairs={{0,2},{2,0},{4,6},{6,4},{8,10},{10,8},{12,14},{14,12},{16,18},{18,... | collective-permute-start | bytes 1769480 | tf_op jit(solution)/shard_map/ppermute | solution.py:86
  475.4 84.1 %collective-permute-start.100 = (bf16[256,768]{1,0:T(8,128)(2,1)S(1)}, bf16[256,768]{1,0:T(8,128)(2,1)S(1)}, u32[]{:S(2)}, u32[]{:S(2)}) collective-permute-start(bf16[256,768]{1,0:T(8,128)(2,1)S(1)} %constant_dynamic-slice_fusion.11), channel_id=1, source_target_pairs={{0,4},{2,6},{4,0},{6,2},{8,12},{10,14},{12,8},{14,10},{16,20},{18,... | collective-permute-start | bytes 1179656 | tf_op jit(solution)/shard_map/ppermute | solution.py:86
  476.6 33.0 %collective-permute-start.108 = (bf16[128,768]{1,0:T(8,128)(2,1)S(1)}, bf16[128,768]{1,0:T(8,128)(2,1)S(1)}, u32[]{:S(2)}, u32[]{:S(2)}) collective-permute-start(bf16[128,768]{1,0:T(8,128)(2,1)S(1)} %constant_dynamic-slice_fusion.7), channel_id=1, source_target_pairs={{0,8},{2,10},{4,12},{6,14},{8,0},{10,2},{12,4},{14,6},{16,24},{18,... | collective-permute-start | bytes 589832 | tf_op jit(solution)/shard_map/ppermute | solution.py:86
  478.7 111.0 %collective-permute-start.67 = (bf16[192,1536]{1,0:T(8,128)(2,1)S(1)}, bf16[192,1536]{1,0:T(8,128)(2,1)S(1)}, u32[]{:S(2)}, u32[]{:S(2)}) collective-permute-start(bf16[192,1536]{1,0:T(8,128)(2,1)S(1)} %constant_dynamic-slice_fusion.28), channel_id=1, source_target_pairs={{0,2},{2,0},{4,6},{6,4},{8,10},{10,8},{12,14},{14,12},{16,18},{18,... | collective-permute-start | bytes 1769480 | tf_op jit(solution)/shard_map/ppermute | solution.py:86
  508.8 45.5 %collective-permute-start.75 = (bf16[128,1536]{1,0:T(8,128)(2,1)S(1)}, bf16[128,1536]{1,0:T(8,128)(2,1)S(1)}, u32[]{:S(2)}, u32[]{:S(2)}) collective-permute-start(bf16[128,1536]{1,0:T(8,128)(2,1)S(1)} %constant_dynamic-slice_fusion.24), channel_id=1, source_target_pairs={{0,4},{2,6},{4,0},{6,2},{8,12},{10,14},{12,8},{14,10},{16,20},{18,... | collective-permute-start | bytes 1179656 | tf_op jit(solution)/shard_map/ppermute | solution.py:86
  553.2 21.6 %collective-permute-start.27 = (bf16[128,1152]{1,0:T(8,128)(2,1)S(1)}, bf16[128,1152]{1,0:T(8,128)(2,1)S(1)}, u32[]{:S(2)}, u32[]{:S(2)}) collective-permute-start(bf16[128,1152]{1,0:T(8,128)(2,1)S(1)} %maximum_select_fusion.15), channel_id=1, source_target_pairs={{0,4},{2,6},{4,0},{6,2},{8,12},{10,14},{12,8},{14,10},{16,20},{18,... | collective-permute-start | bytes 884744 | tf_op jit(solution)/shard_map/ppermute | solution.py:86
  564.4 25.5 %collective-permute-start.101 = (bf16[128,768]{1,0:T(8,128)(2,1)S(1)}, bf16[128,768]{1,0:T(8,128)(2,1)S(1)}, u32[]{:S(2)}, u32[]{:S(2)}) collective-permute-start(bf16[128,768]{1,0:T(8,128)(2,1)S(1)} %constant_dynamic-slice_fusion.10), channel_id=1, source_target_pairs={{0,8},{2,10},{4,12},{6,14},{8,0},{10,2},{12,4},{14,6},{16,24},{18,... | collective-permute-start | bytes 589832 | tf_op jit(solution)/shard_map/ppermute | solution.py:86
  586.3 29.4 %collective-permute-start.115 = (bf16[128,768]{1,0:T(8,128)(2,1)S(1)}, bf16[128,768]{1,0:T(8,128)(2,1)S(1)}, u32[]{:S(2)}, u32[]{:S(2)}) collective-permute-start(bf16[128,768]{1,0:T(8,128)(2,1)S(1)} %maximum_select_fusion.25), channel_id=1, source_target_pairs={{0,8},{2,10},{4,12},{6,14},{8,0},{10,2},{12,4},{14,6},{16,24},{18,... | collective-permute-start | bytes 589832 | tf_op jit(solution)/shard_map/ppermute | solution.py:86
  589.7 25.3 %collective-permute-start.90 = (bf16[64,1536]{1,0:T(8,128)(2,1)S(1)}, bf16[64,1536]{1,0:T(8,128)(2,1)S(1)}, u32[]{:S(2)}, u32[]{:S(2)}) collective-permute-start(bf16[64,1536]{1,0:T(8,128)(2,1)S(1)} %maximum_select_fusion.23), channel_id=1, source_target_pairs={{0,8},{2,10},{4,12},{6,14},{8,0},{10,2},{12,4},{14,6},{16,24},{18,... | collective-permute-start | bytes 589832 | tf_op jit(solution)/shard_map/ppermute | solution.py:86
  589.9 33.1 %collective-permute-start.93 = (bf16[192,768]{1,0:T(8,128)(2,1)S(1)}, bf16[192,768]{1,0:T(8,128)(2,1)S(1)}, u32[]{:S(2)}, u32[]{:S(2)}) collective-permute-start(bf16[192,768]{1,0:T(8,128)(2,1)S(1)} %constant_dynamic-slice_fusion.14), channel_id=1, source_target_pairs={{0,4},{2,6},{4,0},{6,2},{8,12},{10,14},{12,8},{14,10},{16,20},{18,... | collective-permute-start | bytes 884744 | tf_op jit(solution)/shard_map/ppermute | solution.py:86
  591.1 35.6 %collective-permute-start.68 = (bf16[96,1536]{1,0:T(8,128)(2,1)S(1)}, bf16[96,1536]{1,0:T(8,128)(2,1)S(1)}, u32[]{:S(2)}, u32[]{:S(2)}) collective-permute-start(bf16[96,1536]{1,0:T(8,128)(2,1)S(1)} %constant_dynamic-slice_fusion.27), channel_id=1, source_target_pairs={{0,4},{2,6},{4,0},{6,2},{8,12},{10,14},{12,8},{14,10},{16,20},{18,... | collective-permute-start | bytes 884744 | tf_op jit(solution)/shard_map/ppermute | solution.py:86
  626.6 23.5 %collective-permute-start.106 = (bf16[128,768]{1,0:T(8,128)(2,1)S(1)}, bf16[128,768]{1,0:T(8,128)(2,1)S(1)}, u32[]{:S(2)}, u32[]{:S(2)}) collective-permute-start(bf16[128,768]{1,0:T(8,128)(2,1)S(1)} %maximum_select_fusion.24), channel_id=1, source_target_pairs={{0,8},{2,10},{4,12},{6,14},{8,0},{10,2},{12,4},{14,6},{16,24},{18,... | collective-permute-start | bytes 589832 | tf_op jit(solution)/shard_map/ppermute | solution.py:86
  (195 other events, 1351.9 us)

commit v2 on v1

v2 whole, which is shorter than its diff:
```python
from functools import partial

import jax
import jax.numpy as jnp
from jax import lax
from jax.experimental import pallas as pl
from jax.experimental.pallas import tpu as pltpu
from jax.sharding import PartitionSpec as P

D = 768
HEAD_DIM = 64
SEQ_LEN = 512
PAIR = 2 * HEAD_DIM
norm_eps = 1e-06
f32 = jnp.float32
bf16 = jnp.bfloat16
VMEM_BYTES = 58 << 20


def dot(left, right, left_dim=1, right_dim=0):
    return lax.dot_general(
        left, right, (((left_dim,), (right_dim,)), ((), ())), preferred_element_type=f32
    )


def normalise(values):
    centred = values - jnp.mean(values, axis=-1, keepdims=True)
    inverse = lax.rsqrt(jnp.mean(centred * centred, axis=-1, keepdims=True) + norm_eps)
    return centred * inverse, inverse


def norm_back(grad_rows, normed, inverse, gain):
    inner = grad_rows * gain
    centre_part = jnp.mean(inner, axis=-1, keepdims=True)
    slope_part = jnp.mean(inner * normed, axis=-1, keepdims=True)
    return inverse * (inner - centre_part - normed * slope_part)


def as_column(row):
    return jnp.broadcast_to(row, (8, row.shape[1])).T[:, :1]


def add_rows(ref, rows):
    @pl.when(pl.program_id(0) == 0)
    def _():
        ref[...] = jnp.zeros_like(ref)

    for at, values in enumerate(rows):
        ref[at : at + 1, :] += jnp.sum(values, axis=0, keepdims=True)


def gelu_both(pre):
    size = jnp.abs(pre)
    t = 1.0 / (1.0 + size * (0.3275911 * 0.7071067811865476))
    bell = jnp.exp(pre * pre * -0.5)
    tail = t * (
        0.5 * 0.254829592
        + t * (0.5 * -0.284496736 + t * (0.5 * 1.421413741 + t * (0.5 * -1.453152027 + t * (0.5 * 1.061405429))))
    )
    tail = tail * bell
    below = jnp.where(pre >= 0, 1.0 - tail, tail)
    return pre * below, below + pre * bell * 0.3989422804014327


def attend_kernel(
    side, x_ref, seg_ref, valid_ref, wq_a, wq_b, wk_a, wk_b, wv_a, wv_b, bq_ref, bv_ref, wo_a, wo_b, bo_ref,
    q_ref, k_ref, v_ref, p_ref, ctx_ref, mixed_ref, bias_ref,
):
    x = x_ref[...]
    seg = seg_ref[0].astype(f32)
    allowed = (as_column(seg) == seg) & (valid_ref[0] == 1)
    bias_ref[...] = jnp.where(allowed, 0.0, -1e30)
    width = wq_a.shape[1]
    for at, (wq, wk, wv) in enumerate(((wq_a, wk_a, wv_a), (wq_b, wk_b, wv_b))):
        here = slice(at * width, (at + 1) * width)
        q_ref[:, here] = (dot(x, wq[...]) + bq_ref[:, here].astype(f32)).astype(bf16) * jnp.asarray(HEAD_DIM ** -0.5, bf16)
        k_ref[:, here] = dot(x, wk[...]).astype(bf16)
        v_ref[:, here] = (dot(x, wv[...]) + bv_ref[:, here].astype(f32)).astype(bf16)

    lane = lax.broadcasted_iota(jnp.int32, (1, PAIR), 1)

    def pair_step(pair, carry):
        here = pl.ds(pl.multiple_of(pair * PAIR, PAIR), PAIR)
        q, k, v = q_ref[:, here], k_ref[:, here], v_ref[:, here]
        parts = []
        for head in range(2):
            scores = dot(jnp.where(lane // HEAD_DIM == head, q, 0), k, 1, 1) + bias_ref[...]
            shifted = jnp.exp(scores - jnp.max(scores, axis=-1, keepdims=True))
            probs = (shifted * (1.0 / jnp.sum(shifted, axis=-1, keepdims=True))).astype(bf16)
            p_ref[0, 2 * pair + head] = probs
            parts.append(dot(probs, v))
        ctx_ref[:, here] = jnp.where(lane < HEAD_DIM, parts[0], parts[1]).astype(bf16)
        return carry

    lax.fori_loop(0, 2 * width // PAIR, pair_step, 0)
    attn = dot(ctx_ref[:, :width], wo_a[...]) + dot(ctx_ref[:, width:], wo_b[...])
    mixed_ref[...] = x.astype(f32) + attn + bo_ref[...].astype(f32)


def ffn_kernel(
    side, mixed_ref, valid_ref, cot_ref, w1_a, w1_b, b1_ref, w2_a, w2_b, b2_ref, g1_ref, s1_ref, g2_ref, s2_ref,
    low_first_ref, act_ref, slope_ref, out_ref, grad_ref, low_ref, vec_ref,
):
    normed_one, _ = normalise(mixed_ref[...])
    first = normed_one * g1_ref[...].astype(f32) + s1_ref[...].astype(f32)
    low_first = first.astype(bf16)
    low_first_ref[...] = low_first
    second = first + b2_ref[...].astype(f32)
    width = w1_a.shape[1]
    step = 512
    for half, (w1, w2) in enumerate(((w1_a, w2_a), (w1_b, w2_b))):
        for at in range(0, width, step):
            here = slice(half * width + at, half * width + at + step)
            pre = dot(low_first, w1[:, at : at + step]) + b1_ref[:, here].astype(f32)
            act, slope = gelu_both(pre)
            act = act.astype(bf16)
            act_ref[:, here] = act
            slope_ref[:, here] = slope.astype(bf16)
            second += dot(act, w2[at : at + step, :])
    normed_two, inverse_two = normalise(second)
    gain = g2_ref[...].astype(f32)
    out_ref[...] = (normed_two * gain + s2_ref[...].astype(f32)).astype(bf16)
    valid = as_column(valid_ref[0].astype(f32))
    grad_out = cot_ref[...].astype(f32) * valid
    grad = norm_back(grad_out, normed_two, inverse_two, gain)
    grad_ref[...] = grad
    low_ref[...] = grad.astype(bf16)
    add_rows(vec_ref, (grad_out * normed_two, grad_out, grad, grad * grad * valid))


def ffn_back_kernel(
    side, low_ref, grad_ref, slope_ref, mixed_ref, valid_ref, w1_a, w1_b, w2_a, w2_b, wo_a, wo_b, g1_ref,
    pre_ref, mixed_grad_ref, low_mixed_ref, ctx_grad_ref, vec_ref, hidden_ref,
):
    low = low_ref[...]
    grad_first = grad_ref[...]
    width = w1_a.shape[1]
    step = 512

    @pl.when(pl.program_id(0) == 0)
    def _():
        hidden_ref[...] = jnp.zeros_like(hidden_ref)

    for half, (w1, w2) in enumerate(((w1_a, w2_a), (w1_b, w2_b))):
        for at in range(0, width, step):
            here = slice(half * width + at, half * width + at + step)
            grad_pre = (dot(low, w2[at : at + step, :], 1, 1) * slope_ref[:, here].astype(f32)).astype(bf16)
            pre_ref[:, here] = grad_pre
            hidden_ref[:, here] += jnp.sum(grad_pre.astype(f32), axis=0, keepdims=True)
            grad_first += dot(grad_pre, w1[:, at : at + step], 1, 1)
    normed_one, inverse_one = normalise(mixed_ref[...])
    grad_mixed = norm_back(grad_first, normed_one, inverse_one, g1_ref[...].astype(f32))
    mixed_grad_ref[...] = grad_mixed
    low_mixed = grad_mixed.astype(bf16)
    low_mixed_ref[...] = low_mixed
    head_width = wo_a.shape[0]
    ctx_grad_ref[:, :head_width] = dot(low_mixed, wo_a[...], 1, 1).astype(bf16)
    ctx_grad_ref[:, head_width:] = dot(low_mixed, wo_b[...], 1, 1).astype(bf16)
    valid = as_column(valid_ref[0].astype(f32))
    add_rows(
        vec_ref,
        (grad_first * normed_one, grad_first, grad_mixed, grad_first * grad_first * valid, grad_mixed * grad_mixed * valid),
    )


def attend_back_kernel(
    side, q_ref, k_ref, v_ref, p_ref, ctx_ref, ctx_grad_ref, mixed_grad_ref, valid_ref, wq_a, wq_b, wk_a, wk_b, wv_a, wv_b,
    dq_ref, dk_ref, dv_ref, in_grad_ref, vec_ref,
):
    lane = lax.broadcasted_iota(jnp.int32, (1, PAIR), 1)
    width = wq_a.shape[1]

    def pair_step(pair, carry):
        here = pl.ds(pl.multiple_of(pair * PAIR, PAIR), PAIR)
        q, k, v = q_ref[:, here], k_ref[:, here], v_ref[:, here]
        ctx, ctx_grad = ctx_ref[:, here].astype(f32), ctx_grad_ref[:, here]
        dq, dk, dv = [], 0.0, 0.0
        for head in range(2):
            ours = lane // HEAD_DIM == head
            masked = jnp.where(ours, ctx_grad, 0)
            inner = jnp.sum(masked.astype(f32) * ctx, axis=-1, keepdims=True)
            probs = p_ref[0, 2 * pair + head]
            grad_scores = (probs.astype(f32) * (dot(masked, v, 1, 1) - inner)).astype(bf16)
            dq.append(dot(grad_scores, k))
            dk += dot(jnp.where(ours, q, 0), grad_scores, 0, 0)
            dv += dot(masked, probs, 0, 0)
        dq_ref[:, here] = (jnp.where(lane < HEAD_DIM, dq[0], dq[1]) * HEAD_DIM ** -0.5).astype(bf16)
        dk_ref[:, here] = dk.T.astype(bf16)
        dv_ref[:, here] = dv.T.astype(bf16)
        return carry

    lax.fori_loop(0, 2 * width // PAIR, pair_step, 0)
    grad_in = mixed_grad_ref[...]
    for at, weights in enumerate(((wq_a, wk_a, wv_a), (wq_b, wk_b, wv_b))):
        here = slice(at * width, (at + 1) * width)
        for rows, weight in zip((dq_ref, dk_ref, dv_ref), weights):
            grad_in += dot(rows[:, here], weight[...], 1, 1)
    in_grad_ref[...] = grad_in.astype(bf16)
    valid = as_column(valid_ref[0].astype(f32))
    add_rows(vec_ref, (dq_ref[...].astype(f32), dv_ref[...].astype(f32), grad_in * grad_in * valid))


def run_kernel(kernel, grid, side, operands, outs, scratch=(), cost=(0, 0)):
    def spec(block, kind):
        rest = (0,) * (len(block) - 1)
        if kind == "all":
            return pl.BlockSpec(block, lambda i, s: (0,) + rest, pipeline_mode=pl.Buffered(1))
        if kind == "sum":
            return pl.BlockSpec(block, lambda i, s: (0,) + rest)
        if kind == "shared":
            return pl.BlockSpec(block, lambda i, s: (s[0] * grid + i,) + rest)
        return pl.BlockSpec(block, lambda i, s: (i,) + rest)

    return pl.pallas_call(
        kernel,
        grid_spec=pltpu.PrefetchScalarGridSpec(
            num_scalar_prefetch=1,
            grid=(grid,),
            in_specs=[spec(block, kind) for _, block, kind in operands],
            out_specs=[spec(block, kind) for _, block, kind in outs],
            scratch_shapes=list(scratch),
        ),
        out_shape=[shape for shape, _, _ in outs],
        compiler_params=pltpu.CompilerParams(vmem_limit_bytes=VMEM_BYTES),
        cost_estimate=pl.CostEstimate(flops=int(cost[0]), bytes_accessed=int(cost[1]), transcendentals=0),
    )(side, *[array for array, _, _ in operands])


def like(shape, dtype):
    return jax.ShapeDtypeStruct(shape, dtype)


def whole(array):
    return (array, array.shape, "all")


def swap_narrow(values):
    return lax.ppermute(values, "narrow", [(0, 1), (1, 0)])


def swap_wide(values, bit, size):
    return lax.ppermute(values, "wide", [(i, i ^ (1 << bit)) for i in range(size)])


def halve(values, orders, size):
    me = lax.axis_index("wide")
    states = list(values)
    for step in range(len(orders[0])):
        fresh = []
        for state, order in zip(states, orders):
            bit = order[step]
            half = state.shape[0] // 2
            mine = (me >> bit) & 1
            kept = lax.dynamic_slice_in_dim(state, mine * half, half, 0)
            sent = lax.dynamic_slice_in_dim(state, (1 - mine) * half, half, 0)
            got = swap_wide(sent, bit, size)
            fresh.append((kept.astype(f32) + got.astype(f32)).astype(bf16))
        states = fresh
    return states


def double(states, orders, size):
    me = lax.axis_index("wide")
    for step in reversed(range(len(orders[0]))):
        fresh = []
        for state, order in zip(states, orders):
            bit = order[step]
            mine = (me >> bit) & 1
            got = swap_wide(state, bit, size)
            fresh.append(
                jnp.where(
                    mine == 1,
                    jnp.concatenate([got, state], 0),
                    jnp.concatenate([state, got], 0),
                )
            )
        states = fresh
    return states


def sum_wide(values, size):
    bits = size.bit_length() - 1
    if size != 1 << bits or values.shape[0] % (6 * size):
        return lax.psum(values, "wide").astype(f32)
    first = list(range(bits))
    orders = [first]
    if bits >= 3:
        rest = list(range(3, bits))
        orders = [[0, 1, 2] + rest, [1, 2, 0] + rest, [2, 0, 1] + rest]
        sixth = values.shape[0] // 6
        parts = [values[: 3 * sixth], values[3 * sixth : 5 * sixth], values[5 * sixth :]]
    else:
        parts = [values]
    parts = double(halve(parts, orders, size), orders, size)
    return jnp.concatenate(parts, 0).astype(f32)


def sum_small(values, size):
    bits = size.bit_length() - 1
    if size != 1 << bits:
        return lax.psum(values, "wide")
    for bit in range(bits):
        values = values + swap_wide(values, bit, size)
    return values


def body(size, *arrays):
    (
        inputs, segments, valid, w_query, w_key, w_value, b_query, b_value, w_attn_out, b_attn_out,
        gain_one, shift_one, w_ffn_in, b_ffn_in, w_ffn_out, b_ffn_out, gain_two, shift_two, out_grad,
    ) = arrays
    side = lax.axis_index("narrow")
    rows = inputs.shape[0] // 2
    seqs = rows // SEQ_LEN
    head_width = w_query.shape[1]
    hidden = w_ffn_in.shape[1]
    heads = 2 * head_width // HEAD_DIM
    side_ref = side.astype(jnp.int32).reshape(1)
    row_block = 256
    blocks = rows // row_block

    def pair_of(array):
        return (array, swap_narrow(array))

    def join_rows(array):
        other = swap_narrow(array)
        return jnp.where(
            side == 0,
            jnp.concatenate([array, other], 0),
            jnp.concatenate([other, array], 0),
        )

    def line(array):
        return array.reshape(1, -1)

    wq, wk, wv = pair_of(w_query), pair_of(w_key), pair_of(w_value)
    small_own = jnp.concatenate([b_query, b_value, b_ffn_in])
    small_other = swap_narrow(small_own)
    bq = jnp.concatenate([b_query, small_other[:head_width]])
    bv = jnp.concatenate([b_value, small_other[head_width : 2 * head_width]])
    b1 = jnp.concatenate([b_ffn_in, small_other[2 * head_width :]])
    wo, w1, w2 = pair_of(w_attn_out), pair_of(w_ffn_in), pair_of(w_ffn_out)
    seg_rows = segments.reshape(-1, 1, SEQ_LEN)
    valid_seq = valid.reshape(-1, 1, SEQ_LEN)
    valid_block = valid.reshape(-1, 1, row_block)
    seq = (SEQ_LEN, D)
    blk = (row_block, D)
    wide_blk = (row_block, 2 * hidden)
    low_rows = like((rows, D), bf16)
    full_rows = like((rows, D), f32)

    queries, keys, values, probs, context, mixed = run_kernel(
        attend_kernel,
        seqs,
        side_ref,
        [(inputs, seq, "shared"), (seg_rows, (1, 1, SEQ_LEN), "shared"), (valid_seq, (1, 1, SEQ_LEN), "shared")]
        + [whole(w) for w in wq + wk + wv]
        + [whole(line(bq)), whole(line(bv))]
        + [whole(w) for w in wo]
        + [whole(line(b_attn_out))],
        [(low_rows, seq, "own")] * 3
        + [(like((seqs, heads, SEQ_LEN, SEQ_LEN), bf16), (1, heads, SEQ_LEN, SEQ_LEN), "own")]
        + [(low_rows, seq, "own"), (full_rows, seq, "own")],
        [pltpu.VMEM((SEQ_LEN, SEQ_LEN), f32)],
        (rows * D * D * 8 + rows * SEQ_LEN * D * 4, rows * D * 16),
    )
    low_first, activated, slope, final, grad_second, low_second, vec_two = run_kernel(
        ffn_kernel,
        blocks,
        side_ref,
        [(mixed, blk, "own"), (valid_block, (1, 1, row_block), "shared"), (out_grad, blk, "shared")]
        + [whole(w) for w in w1]
        + [whole(line(b1))]
        + [whole(w) for w in w2]
        + [whole(line(v)) for v in (b_ffn_out, gain_one, shift_one, gain_two, shift_two)],
        [
            (low_rows, blk, "own"),
            (like((rows, 2 * hidden), bf16), wide_blk, "own"),
            (like((rows, 2 * hidden), bf16), wide_blk, "own"),
            (low_rows, blk, "own"),
            (full_rows, blk, "own"),
            (low_rows, blk, "own"),
            (like((8, D), f32), (8, D), "sum"),
        ],
        (),
        (rows * D * hidden * 8, rows * D * 30),
    )
    output = join_rows(final)

    def shared_sum(sent, kept):
        return sum_wide((kept + swap_narrow(sent.astype(bf16)).astype(f32)).astype(bf16), size)

    d_w_ffn_out = shared_sum(
        dot(activated[:, hidden:], low_second, 0, 0), dot(activated[:, :hidden], low_second, 0, 0)
    )
    grad_pre, grad_mixed, low_mixed, grad_context, vec_one, vec_hidden = run_kernel(
        ffn_back_kernel,
        blocks,
        side_ref,
        [
            (low_second, blk, "own"),
            (grad_second, blk, "own"),
            (slope, wide_blk, "own"),
            (mixed, blk, "own"),
            (valid_block, (1, 1, row_block), "shared"),
        ]
        + [whole(w) for w in w1 + w2 + wo]
        + [whole(line(gain_one))],
        [
            (like((rows, 2 * hidden), bf16), wide_blk, "own"),
            (full_rows, blk, "own"),
            (low_rows, blk, "own"),
            (low_rows, blk, "own"),
            (like((8, D), f32), (8, D), "sum"),
            (like((1, 2 * hidden), f32), (1, 2 * hidden), "sum"),
        ],
        (),
        (rows * D * hidden * 8, rows * D * 30),
    )
    d_w_ffn_in = shared_sum(
        dot(low_first, grad_pre[:, hidden:], 0, 0), dot(low_first, grad_pre[:, :hidden], 0, 0)
    )
    d_w_attn_out = shared_sum(
        dot(context[:, head_width:], low_mixed, 0, 0), dot(context[:, :head_width], low_mixed, 0, 0)
    )
    grad_queries, grad_keys, grad_values, grad_in, vec_in = run_kernel(
        attend_back_kernel,
        seqs,
        side_ref,
        [(a, seq, "own") for a in (queries, keys, values)]
        + [(probs, (1, heads, SEQ_LEN, SEQ_LEN), "own")]
        + [(a, seq, "own") for a in (context, grad_context, grad_mixed)]
        + [(valid_seq, (1, 1, SEQ_LEN), "shared")]
        + [whole(w) for w in wq + wk + wv],
        [(low_rows, seq, "own")] * 4 + [(like((8, D), f32), (8, D), "sum")],
        (),
        (rows * D * D * 6 + rows * SEQ_LEN * D * 8, rows * D * 30),
    )
    input_grad = join_rows(grad_in)
    own_rows = lax.dynamic_slice_in_dim(inputs, side * rows, rows, 0)
    three = (grad_queries, grad_keys, grad_values)
    d_w_three = shared_sum(
        dot(own_rows, jnp.concatenate([g[:, head_width:] for g in three], 1), 0, 0),
        dot(own_rows, jnp.concatenate([g[:, :head_width] for g in three], 1), 0, 0),
    )

    count = jnp.sum(lax.dynamic_slice_in_dim(valid, side * rows, rows, 0).astype(f32))
    halves = jnp.concatenate(
        [vec_in[0, :head_width], vec_in[1, :head_width], vec_hidden[0, :hidden]]
        + [vec_in[0, head_width:], vec_in[1, head_width:], vec_hidden[0, hidden:]]
    )
    stats = jnp.stack([jnp.sum(v) for v in (vec_in[2], vec_two[3], vec_one[3], vec_one[4])] + [count])
    rest = jnp.concatenate(
        [vec_one[2], vec_one[0], vec_one[1], vec_two[2], vec_two[0], vec_two[1], jnp.pad(stats, (0, 128 - 5))]
    )
    split = halves.shape[0] // 2
    moved = swap_narrow(jnp.concatenate([halves[split:], rest]))
    small = jnp.concatenate([halves[:split], rest]) + moved
    small = sum_small(small, size)
    ends = []
    at = 0
    for length in (head_width, head_width, hidden) + (D,) * 6 + (128,):
        ends.append(small[at : at + length])
        at += length
    rms = jnp.sqrt(ends[9][:4] / (ends[9][4] * D))
    return (
        output,
        input_grad,
        d_w_three[:, :head_width],
        d_w_three[:, head_width : 2 * head_width],
        d_w_three[:, 2 * head_width :],
        ends[0],
        ends[1],
        d_w_attn_out,
        ends[3],
        ends[4],
        ends[5],
        d_w_ffn_in,
        ends[2],
        d_w_ffn_out,
        ends[6],
        ends[7],
        ends[8],
        rms,
    )


def solution(mesh):
    row, col = P("narrow", None), P(None, "narrow")
    one, rows = P("narrow"), P("wide", None)
    in_specs = (
        rows, P("wide"), P("wide"), col, col, col, one, one, row, P(), P(), P(), col, one, row, P(), P(), P(), rows,
    )
    out_specs = (
        rows, rows, col, col, col, one, one, row, P(), P(), P(), col, one, row, P(), P(), P(), P(),
    )
    return jax.shard_map(
        partial(body, mesh.shape["wide"]), mesh=mesh, in_specs=in_specs, out_specs=out_specs, check_vma=False
    )
```

time: 685 us -> 538 us (0.79)
  matrix products: 173 us -> 20.2 us
  Pallas kernels: 0 us -> 114 us
  local copies, waits for them, and re-layouts: 101 us -> 21 us
  other arithmetic: 54.6 us -> 22.6 us
  starting transfers between devices: 113 us -> 138 us
  waiting for transfers between devices: 230 us -> 211 us
    dot_general x34 -> x8, matrix products: 173 us -> 20.2 us  [dot(): lax.dot_general(left, right, (((left_dim,), (right_dim,)), ((), ())), pre...]
    pallas_call x0 -> x4, Pallas kernels: none -> 114 us  [run_kernel(): pl.pallas_call(kernel, grid_spec=pltpu.PrefetchScalarGridSpec(num_scalar_...]
    unnamed x201 -> x52, local copies, waits for them, and re-layouts: 36.6 us -> 1.3 us
    ppermute x100, starting transfers between devices: 109 us -> 134 us  [swap_wide(): lax.ppermute(values, 'wide', [(i, i ^ 1 << bit) for i in range(size)])]
    while x32 -> x0, local copies, waits for them, and re-layouts: 20.5 us -> none  [the longest x4 10.4 us: body(): grads = lax.map(partial(attend_backward, scale=scale), back_inputs)]
    ppermute x100, waiting for transfers between devices: 228 us -> 208 us  [swap_wide(): lax.ppermute(values, 'wide', [(i, i ^ 1 << bit) for i in range(size)])]
    convert_element_type x13 -> x0, other arithmetic: 18.9 us -> none  [the longest x2 14.2 us: attend_backward(): grad_scores = (probs * centred).astype(bf16)]
    reduce_sum x10 -> x4, other arithmetic: 18.6 us -> 3.95 us  [the longest x3 2.58 us: body(): jnp.sum(v)]
  transfers between devices with their start and end apart: 116 -> 114, of which waited for: 69 -> 71; matrix products, arithmetic and copies ran while one was open for 24% -> 10% of each run, Pallas kernels for 0% -> 6%
where the time goes in v2:
time: 538 us; the launch traced here: 530 us
  waiting for transfers between devices  211 us (39%)
  starting transfers between devices  138 us (26%)
  Pallas kernels  114 us (21%)
  other arithmetic  22.6 us (4%)
  local copies, waits for them, and re-layouts  21 us (4%)
  matrix products  20.2 us (4%)
    ppermute x100, waiting for transfers between devices, swap_wide(): lax.ppermute(values, 'wide', [(i, i ^ 1 << bit) for i in range(size)])  208 us
    ppermute x100, starting transfers between devices, swap_wide(): lax.ppermute(values, 'wide', [(i, i ^ 1 << bit) for i in range(size)])  134 us
    pallas_call x4, Pallas kernels, run_kernel(): pl.pallas_call(kernel, grid_spec=pltpu.PrefetchScalarGridSpec(num_scalar_...  114 us
    dot_general x8, matrix products, dot(): lax.dot_general(left, right, (((left_dim,), (right_dim,)), ((), ())), pre...  20.2 us
  transfers between devices with their start and end apart: 114, of which 71 were waited for; matrix products, arithmetic and copies ran while one was open for 10% of the time, Pallas kernels for 6%

profile of v2, /device:TPU:0, one launch (start us, length us, event | category | flops | bytes accessed | tf_op | source)
XLA Modules:
  0.0 529.8 jit_solution(5303113296167059080)
XLA Ops:
  21.0 29.4 %shard_map.322 = (bf16[1024,768]{1,0:T(8,128)(2,1)}, bf16[1024,768]{1,0:T(8,128)(2,1)}, bf16[1024,768]{1,0:T(8,128)(2,1)}, bf16[2,12,512,512]{3,2,1,0:T(8,128)(2...) custom-call(s32[1]{0:T(128)} %bitcast.side, bf16[2048,768]{1,0:T(8,128)(2,1)} %x_ref.1, s32[4,1,512]{2,1,0:T(1,128)} %bitcast.20, ...), custom_call_target="tpu_custom_call" | custom-call | flops 6442450944 | bytes 12582912 | tf_op jit(solution)/shard_map/pallas_call | solution.py:214
  50.4 30.4 %shard_map.323 = (bf16[1024,768]{1,0:T(8,128)(2,1)}, bf16[1024,3072]{1,0:T(8,128)(2,1)}, bf16[1024,3072]{1,0:T(8,128)(2,1)}, bf16[1024,768]{1,0:T(8,128)(2,1)}, ...) custom-call(s32[1]{0:T(128)} %bitcast.side, f32[1024,768]{1,0:T(8,128)} %get-tuple-element.42.mixed_ref, ...), custom_call_target="tpu_custom_call" | custom-call | flops 9663676416 | bytes 23592960 | tf_op jit(solution)/shard_map/pallas_call | solution.py:214
  80.8 25.2 %shard_map.324 = (bf16[1024,3072]{1,0:T(8,128)(2,1)}, f32[1024,768]{1,0:T(8,128)}, bf16[1024,768]{1,0:T(8,128)(2,1)}, bf16[1024,768]{1,0:T(8,128)(2,1)}, f32[8,768]{1,0:T(8,128)}, /*index=5*/f32[1,3072]{1,0:T(1,128)}) custom-call(s32[1]{0:T(128)} %bitcast.side, bf16[1024,768]{1,0:T(8,128)(2,1)} %get-tuple-element.49.low_ref, ...), custom_call_target="tpu_custom_call" | custom-call | flops 9663676416 | bytes 23592960 | tf_op jit(solution)/shard_map/pallas_call | solution.py:214
  106.0 29.0 %shard_map.325 = (bf16[1024,768]{1,0:T(8,128)(2,1)}, bf16[1024,768]{1,0:T(8,128)(2,1)}, bf16[1024,768]{1,0:T(8,128)(2,1)}, bf16[1024,768]{1,0:T(8,128)(2,1)}, f32[8,768]{1,0:T(8,128)}) custom-call(s32[1]{0:T(128)} %bitcast.side, bf16[1024,768]{1,0:T(8,128)(2,1)} %get-tuple-element.44.q_ref, bf16[1024,768]{1,0:T(8,128)(2,1)} %get-tuple-element.45.k_ref, ...), custom_call_target="tpu_custom_call" | custom-call | flops 6845104128 | bytes 23592960 | tf_op jit(solution)/shard_map/pallas_call | solution.py:214
  142.3 4.7 convolution_convert_fusion
  210.3 3.6 collective-permute-done.40
  335.8 14.8 %collective-permute-done.23 = bf16[32,1152]{1,0:T(8,128)(2,1)S(1)} collective-permute-done((bf16[32,1152]{1,0:T(8,128)(2,1)S(1)}, bf16[32,1152]{1,0:T(8,128)(2,1)S(1)}, u32[]{:S(2)}, u32[]{:S(2)}) %collective-permute-start.23) | collective-permute-done | bytes 73760 | tf_op jit(solution)/shard_map/ppermute | solution.py:242
  350.8 5.1 collective-permute-done.12
  356.0 5.6 %collective-permute-done.81 = bf16[64,1536]{1,0:T(8,128)(2,1)S(1)} collective-permute-done((bf16[64,1536]{1,0:T(8,128)(2,1)S(1)}, bf16[64,1536]{1,0:T(8,128)(2,1)S(1)}, u32[]{:S(2)}, u32[]{:S(2)}) %collective-permute-start.81) | collective-permute-done | bytes 196640 | tf_op jit(solution)/shard_map/ppermute | solution.py:242
  363.6 4.8 collective-permute-done.13
  368.5 5.1 collective-permute-done.24
  373.8 4.8 collective-permute-done.14
  379.3 4.0 collective-permute-done.107
  383.9 4.0 collective-permute-done.82
  388.4 3.6 collective-permute-done.108
  396.4 4.4 collective-permute-done.109
  401.4 4.3 collective-permute-done.84
  407.8 3.7 collective-permute-done.85
  433.1 4.5 collective-permute-done.87
  456.1 5.0 collective-permute-done.76
  461.5 4.9 collective-permute-done.101
  505.4 3.6 collective-permute-done.96
  510.7 5.7 %collective-permute-done.71 = bf16[96,1536]{1,0:T(8,128)(2,1)S(1)} collective-permute-done((bf16[96,1536]{1,0:T(8,128)(2,1)S(1)}, bf16[96,1536]{1,0:T(8,128)(2,1)S(1)}, u32[]{:S(2)}, u32[]{:S(2)}) %collective-permute-start.71) | collective-permute-done | bytes 294944 | tf_op jit(solution)/shard_map/ppermute | solution.py:242
  522.2 4.3 collective-permute-done.72
  (469 shorter events, 312.3 us)
Async XLA Ops:
  0.7 49.7 %collective-permute-start.5 = (bf16[768,1536]{1,0:T(8,128)(2,1)}, bf16[768,1536]{1,0:T(8,128)(2,1)}, u32[]{:S(2)}, u32[]{:S(2)}) collective-permute-start(bf16[768,1536]{1,0:T(8,128)(2,1)} %w1_a.3), channel_id=1, source_target_pairs={{0,1},{1,0},{2,3},{3,2},{4,5},{5,4},{6,7},{7,6},{8,9},{9,8},{10,11... | collective-permute-start | bytes 7077896 | tf_op jit(solution)/shard_map/ppermute | solution.py:238
  1.2 49.2 %collective-permute-start.6 = (bf16[1536,768]{1,0:T(8,128)(2,1)}, bf16[1536,768]{1,0:T(8,128)(2,1)}, u32[]{:S(2)}, u32[]{:S(2)}) collective-permute-start(bf16[1536,768]{1,0:T(8,128)(2,1)} %w2_a.3), channel_id=1, source_target_pairs={{0,1},{1,0},{2,3},{3,2},{4,5},{5,4},{6,7},{7,6},{8,9},{9,8},{10,11... | collective-permute-start | bytes 7077896 | tf_op jit(solution)/shard_map/ppermute | solution.py:238
  2.5 17.2 %collective-permute-start.1 = (bf16[768,384]{1,0:T(8,128)(2,1)}, bf16[768,384]{1,0:T(8,128)(2,1)S(1)}, u32[]{:S(2)}, u32[]{:S(2)}) collective-permute-start(bf16[768,384]{1,0:T(8,128)(2,1)} %wk_a.3), channel_id=1, source_target_pairs={{0,1},{1,0},{2,3},{3,2},{4,5},{5,4},{6,7},{7,6},{8,9},{9,8},{10,11... | collective-permute-start | bytes 1769480 | tf_op jit(solution)/shard_map/ppermute | solution.py:238
  147.0 175.4 %collective-permute-start.89 = (bf16[1536,768]{1,0:T(8,128)(2,1)S(1)}, bf16[1536,768]{1,0:T(8,128)(2,1)S(1)}, u32[]{:S(2)}, u32[]{:S(2)}) collective-permute-start(bf16[1536,768]{1,0:T(8,128)(2,1)S(1)} %convolution_convert_fusion), channel_id=1, source_target_pairs={{0,1},{1,0},{2,3},{3,2},{4,5},{5,4},{6,7},{7,6},{8,9},{9,8},{10,11... | collective-permute-start | bytes 7077896 | tf_op jit(solution)/shard_map/ppermute | solution.py:238
  150.8 174.9 %collective-permute-start.64 = (bf16[768,1536]{1,0:T(8,128)(2,1)S(1)}, bf16[768,1536]{1,0:T(8,128)(2,1)S(1)}, u32[]{:S(2)}, u32[]{:S(2)}) collective-permute-start(bf16[768,1536]{1,0:T(8,128)(2,1)S(1)} %convolution_convert_fusion.1), channel_id=1, source_target_pairs={{0,1},{1,0},{2,3},{3,2},{4,5},{5,4},{6,7},{7,6},{8,9},{9,8},{10,11... | collective-permute-start | bytes 7077896 | tf_op jit(solution)/shard_map/ppermute | solution.py:238
  151.9 18.7 %collective-permute-start.39 = (bf16[384,768]{1,0:T(8,128)(2,1)S(1)}, bf16[384,768]{1,0:T(8,128)(2,1)S(1)}, u32[]{:S(2)}, u32[]{:S(2)}) collective-permute-start(bf16[384,768]{1,0:T(8,128)(2,1)S(1)} %convolution_convert_fusion.3), channel_id=1, source_target_pairs={{0,1},{1,0},{2,3},{3,2},{4,5},{5,4},{6,7},{7,6},{8,9},{9,8},{10,11... | collective-permute-start | bytes 1769480 | tf_op jit(solution)/shard_map/ppermute | solution.py:238
  170.0 99.9 %collective-permute-start.9 = (bf16[768,1152]{1,0:T(8,128)(2,1)S(1)}, bf16[768,1152]{1,0:T(8,128)(2,1)S(1)}, u32[]{:S(2)}, u32[]{:S(2)}) collective-permute-start(bf16[768,1152]{1,0:T(8,128)(2,1)S(1)} %convolution_convert_fusion.2), channel_id=1, source_target_pairs={{0,1},{1,0},{2,3},{3,2},{4,5},{5,4},{6,7},{7,6},{8,9},{9,8},{10,11... | collective-permute-start | bytes 5308424 | tf_op jit(solution)/shard_map/ppermute | solution.py:238
  170.1 113.5 %collective-permute-start.8 = (bf16[1024,768]{1,0:T(8,128)(2,1)S(1)}, bf16[1024,768]{1,0:T(8,128)(2,1)S(1)}, u32[]{:S(2)}, u32[]{:S(2)}) collective-permute-start(bf16[1024,768]{1,0:T(8,128)(2,1)S(1)} %copy-done.5), channel_id=1, source_target_pairs={{0,1},{1,0},{2,3},{3,2},{4,5},{5,4},{6,7},{7,6},{8,9},{9,8},{10,11... | collective-permute-start | bytes 4718600 | tf_op jit(solution)/shard_map/ppermute | solution.py:238
  269.8 18.1 %collective-permute-start.7 = (bf16[1024,768]{1,0:T(8,128)(2,1)S(1)}, bf16[1024,768]{1,0:T(8,128)(2,1)S(1)}, u32[]{:S(2)}, u32[]{:S(2)}) collective-permute-start(bf16[1024,768]{1,0:T(8,128)(2,1)S(1)} %copy-done.4), channel_id=1, source_target_pairs={{0,1},{1,0},{2,3},{3,2},{4,5},{5,4},{6,7},{7,6},{8,9},{9,8},{10,11... | collective-permute-start | bytes 4718600 | tf_op jit(solution)/shard_map/ppermute | solution.py:238
  317.5 17.5 %collective-permute-start.11 = (bf16[96,1152]{1,0:T(8,128)(2,1)S(1)}, bf16[96,1152]{1,0:T(8,128)(2,1)S(1)}, u32[]{:S(2)}, u32[]{:S(2)}) collective-permute-start(bf16[96,1152]{1,0:T(8,128)(2,1)S(1)} %constant_dynamic-slice_fusion.55), channel_id=1, source_target_pairs={{0,4},{2,6},{4,0},{6,2},{8,12},{10,14},{12,8},{14,10},{16,20},{18,... | collective-permute-start | bytes 663560 | tf_op jit(solution)/shard_map/ppermute | solution.py:242
  328.9 109.7 %collective-permute-start.90 = (bf16[384,768]{1,0:T(8,128)(2,1)S(1)}, bf16[384,768]{1,0:T(8,128)(2,1)S(1)}, u32[]{:S(2)}, u32[]{:S(2)}) collective-permute-start(bf16[384,768]{1,0:T(8,128)(2,1)S(1)} %constant_dynamic-slice_fusion.12), channel_id=1, source_target_pairs={{0,2},{2,0},{4,6},{6,4},{8,10},{10,8},{12,14},{14,12},{16,18},{18,... | collective-permute-start | bytes 1769480 | tf_op jit(solution)/shard_map/ppermute | solution.py:242
  330.2 81.4 %collective-permute-start.98 = (bf16[256,768]{1,0:T(8,128)(2,1)S(1)}, bf16[256,768]{1,0:T(8,128)(2,1)S(1)}, u32[]{:S(2)}, u32[]{:S(2)}) collective-permute-start(bf16[256,768]{1,0:T(8,128)(2,1)S(1)} %constant_dynamic-slice_fusion.8), channel_id=1, source_target_pairs={{0,4},{2,6},{4,0},{6,2},{8,12},{10,14},{12,8},{14,10},{16,20},{18,... | collective-permute-start | bytes 1179656 | tf_op jit(solution)/shard_map/ppermute | solution.py:242
  331.5 31.3 %collective-permute-start.106 = (bf16[128,768]{1,0:T(8,128)(2,1)S(1)}, bf16[128,768]{1,0:T(8,128)(2,1)S(1)}, u32[]{:S(2)}, u32[]{:S(2)}) collective-permute-start(bf16[128,768]{1,0:T(8,128)(2,1)S(1)} %constant_dynamic-slice_fusion.4), channel_id=1, source_target_pairs={{0,8},{2,10},{4,12},{6,14},{8,0},{10,2},{12,4},{14,6},{16,24},{18,... | collective-permute-start | bytes 589832 | tf_op jit(solution)/shard_map/ppermute | solution.py:242
  333.5 108.1 %collective-permute-start.65 = (bf16[192,1536]{1,0:T(8,128)(2,1)S(1)}, bf16[192,1536]{1,0:T(8,128)(2,1)S(1)}, u32[]{:S(2)}, u32[]{:S(2)}) collective-permute-start(bf16[192,1536]{1,0:T(8,128)(2,1)S(1)} %constant_dynamic-slice_fusion.25), channel_id=1, source_target_pairs={{0,2},{2,0},{4,6},{6,4},{8,10},{10,8},{12,14},{14,12},{16,18},{18,... | collective-permute-start | bytes 1769480 | tf_op jit(solution)/shard_map/ppermute | solution.py:242
  361.6 45.1 %collective-permute-start.73 = (bf16[128,1536]{1,0:T(8,128)(2,1)S(1)}, bf16[128,1536]{1,0:T(8,128)(2,1)S(1)}, u32[]{:S(2)}, u32[]{:S(2)}) collective-permute-start(bf16[128,1536]{1,0:T(8,128)(2,1)S(1)} %constant_dynamic-slice_fusion.21), channel_id=1, source_target_pairs={{0,4},{2,6},{4,0},{6,2},{8,12},{10,14},{12,8},{14,10},{16,20},{18,... | collective-permute-start | bytes 1179656 | tf_op jit(solution)/shard_map/ppermute | solution.py:242
  405.7 21.5 %collective-permute-start.25 = (bf16[128,1152]{1,0:T(8,128)(2,1)S(1)}, bf16[128,1152]{1,0:T(8,128)(2,1)S(1)}, u32[]{:S(2)}, u32[]{:S(2)}) collective-permute-start(bf16[128,1152]{1,0:T(8,128)(2,1)S(1)} %maximum_select_fusion.15), channel_id=1, source_target_pairs={{0,4},{2,6},{4,0},{6,2},{8,12},{10,14},{12,8},{14,10},{16,20},{18,... | collective-permute-start | bytes 884744 | tf_op jit(solution)/shard_map/ppermute | solution.py:242
  416.5 25.3 %collective-permute-start.99 = (bf16[128,768]{1,0:T(8,128)(2,1)S(1)}, bf16[128,768]{1,0:T(8,128)(2,1)S(1)}, u32[]{:S(2)}, u32[]{:S(2)}) collective-permute-start(bf16[128,768]{1,0:T(8,128)(2,1)S(1)} %constant_dynamic-slice_fusion.7), channel_id=1, source_target_pairs={{0,8},{2,10},{4,12},{6,14},{8,0},{10,2},{12,4},{14,6},{16,24},{18,... | collective-permute-start | bytes 589832 | tf_op jit(solution)/shard_map/ppermute | solution.py:242
  438.6 29.5 %collective-permute-start.113 = (bf16[128,768]{1,0:T(8,128)(2,1)S(1)}, bf16[128,768]{1,0:T(8,128)(2,1)S(1)}, u32[]{:S(2)}, u32[]{:S(2)}) collective-permute-start(bf16[128,768]{1,0:T(8,128)(2,1)S(1)} %maximum_select_fusion.25), channel_id=1, source_target_pairs={{0,8},{2,10},{4,12},{6,14},{8,0},{10,2},{12,4},{14,6},{16,24},{18,... | collective-permute-start | bytes 589832 | tf_op jit(solution)/shard_map/ppermute | solution.py:242
  441.6 25.7 %collective-permute-start.88 = (bf16[64,1536]{1,0:T(8,128)(2,1)S(1)}, bf16[64,1536]{1,0:T(8,128)(2,1)S(1)}, u32[]{:S(2)}, u32[]{:S(2)}) collective-permute-start(bf16[64,1536]{1,0:T(8,128)(2,1)S(1)} %maximum_select_fusion.23), channel_id=1, source_target_pairs={{0,8},{2,10},{4,12},{6,14},{8,0},{10,2},{12,4},{14,6},{16,24},{18,... | collective-permute-start | bytes 589832 | tf_op jit(solution)/shard_map/ppermute | solution.py:242
  441.8 32.9 %collective-permute-start.91 = (bf16[192,768]{1,0:T(8,128)(2,1)S(1)}, bf16[192,768]{1,0:T(8,128)(2,1)S(1)}, u32[]{:S(2)}, u32[]{:S(2)}) collective-permute-start(bf16[192,768]{1,0:T(8,128)(2,1)S(1)} %constant_dynamic-slice_fusion.11), channel_id=1, source_target_pairs={{0,4},{2,6},{4,0},{6,2},{8,12},{10,14},{12,8},{14,10},{16,20},{18,... | collective-permute-start | bytes 884744 | tf_op jit(solution)/shard_map/ppermute | solution.py:242
  443.2 35.3 %collective-permute-start.66 = (bf16[96,1536]{1,0:T(8,128)(2,1)S(1)}, bf16[96,1536]{1,0:T(8,128)(2,1)S(1)}, u32[]{:S(2)}, u32[]{:S(2)}) collective-permute-start(bf16[96,1536]{1,0:T(8,128)(2,1)S(1)} %constant_dynamic-slice_fusion.24), channel_id=1, source_target_pairs={{0,4},{2,6},{4,0},{6,2},{8,12},{10,14},{12,8},{14,10},{16,20},{18,... | collective-permute-start | bytes 884744 | tf_op jit(solution)/shard_map/ppermute | solution.py:242
  466.4 20.3 %collective-permute-start.17 = (bf16[192,1152]{1,0:T(8,128)(2,1)S(1)}, bf16[192,1152]{1,0:T(8,128)(2,1)S(1)}, u32[]{:S(2)}, u32[]{:S(2)}) collective-permute-start(bf16[192,1152]{1,0:T(8,128)(2,1)S(1)} %maximum_select_fusion.10), channel_id=1, source_target_pairs={{0,2},{2,0},{4,6},{6,4},{8,10},{10,8},{12,14},{14,12},{16,18},{18,... | collective-permute-start | bytes 1327112 | tf_op jit(solution)/shard_map/ppermute | solution.py:242
  478.4 24.0 %collective-permute-start.104 = (bf16[128,768]{1,0:T(8,128)(2,1)S(1)}, bf16[128,768]{1,0:T(8,128)(2,1)S(1)}, u32[]{:S(2)}, u32[]{:S(2)}) collective-permute-start(bf16[128,768]{1,0:T(8,128)(2,1)S(1)} %maximum_select_fusion.24), channel_id=1, source_target_pairs={{0,8},{2,10},{4,12},{6,14},{8,0},{10,2},{12,4},{14,6},{16,24},{18,... | collective-permute-start | bytes 589832 | tf_op jit(solution)/shard_map/ppermute | solution.py:242
  489.1 21.4 %collective-permute-start.80 = (bf16[128,1536]{1,0:T(8,128)(2,1)S(1)}, bf16[128,1536]{1,0:T(8,128)(2,1)S(1)}, u32[]{:S(2)}, u32[]{:S(2)}) collective-permute-start(bf16[128,1536]{1,0:T(8,128)(2,1)S(1)} %maximum_select_fusion.11), channel_id=1, source_target_pairs={{0,4},{2,6},{4,0},{6,2},{8,12},{10,14},{12,8},{14,10},{16,20},{18,... | collective-permute-start | bytes 1179656 | tf_op jit(solution)/shard_map/ppermute | solution.py:242
  (110 other events, 903.2 us)
